TPU v7x, 512 devices: a whole 4x4x16 slice. The times are simulated.
512 devices in a mesh: ctx: 64 (over z, x), head: 8 (over y, core).
Axes of the slice: x: 4, y: 4, z: 16, core: 2. Of those that a mesh axis runs over, the one named last changes fastest.
Arguments:
- inputs: bfloat16 [32768, 4096], P('ctx', 'head'), may hold values from -6 to 6
- w_in: bfloat16 [4096, 4096], P('ctx', 'head'), may hold values from -0.09375 to 0.09375
- b_rows: bfloat16 [32768, 128], P('ctx'), may hold values from -0.5 to 0.5
- c_rows: bfloat16 [32768, 128], P('ctx'), may hold values from -0.5 to 0.5
- log_decay: float32 [64, 32768], P('head', 'ctx'), may hold values from -2.09375 to 0, as said below
- skip_gain: float32 [64], P('head'), may hold values from 0.5 to 2
- grad_out: bfloat16 [32768, 4096], P('ctx', 'head'), may hold values from -6 to 6
Outputs:
- grad_inputs: bfloat16 [32768, 4096], P('ctx', 'head')
- grad_b: float32 [32768, 128], P('ctx')
- grad_c: float32 [32768, 128], P('ctx')
- grad_log_decay: float32 [64, 32768], P('head', 'ctx')
Inputs may be any that keep to these rules, and one draw needn't show every extreme that they name: log_decay is negative.
All inputs are finite; a program needn't handle non-finite values.
Results may differ from a plain program's by a relative error of at most 0.017.
Values may be sent and summed in bfloat16 or wider, within the bound.
A program may use at most 128 MiB of HBM per device.

v0:
```python
import jax
import jax.numpy as jnp
from jax import lax
from jax.sharding import PartitionSpec as P

SPAN = 256
SPANS_DEV = 2


exact_precision = lax.Precision.HIGHEST


def entering(part, axis, combine, identity, reverse):
    count = lax.axis_size(axis)
    place = lax.axis_index(axis)
    ahead = count - 1 - place if reverse else place
    gathered = jax.tree.map(lambda a: lax.all_gather(a, axis), part)
    state = jax.tree.map(lambda a, e: jnp.zeros_like(a) + jnp.asarray(e, a.dtype), part, identity)

    def one(lap, state):
        source = count - 1 - lap if reverse else lap
        return combine(
            state, jax.tree.map(lambda a: lax.dynamic_index_in_dim(a, source, 0, False), gathered)
        )

    return lax.fori_loop(0, ahead, one, state)


def span_state(x_rows, b_rows, log_decay):
    length = x_rows.shape[0]
    heads = log_decay.shape[0]
    x_heads = x_rows.reshape(length, heads, -1)
    running = jnp.cumsum(log_decay, axis=1)
    to_end = jnp.exp(running[:, -1:] - running)
    own_state = jnp.einsum(
        "shp,sn->hpn", x_heads * to_end.T[:, :, None], b_rows, precision=exact_precision
    )
    return (jnp.exp(running[:, -1]), own_state)


def span_forward(x_rows, b_rows, c_rows, log_decay, state_in, skip_gain):
    length = x_rows.shape[0]
    heads = log_decay.shape[0]
    x_heads = x_rows.reshape(length, heads, -1)
    running = jnp.cumsum(log_decay, axis=1)
    later = lax.broadcasted_iota(jnp.int32, (length, length), 0)
    earlier = lax.broadcasted_iota(jnp.int32, (length, length), 1)
    causal = (later >= earlier)[None]
    spread = running[:, :, None] - running[:, None, :]
    kernel = jnp.where(causal, jnp.exp(jnp.where(causal, spread, 0.0)), 0.0)
    scores = jnp.dot(c_rows, b_rows.T, precision=exact_precision)
    inner = jnp.einsum("hts,shp->thp", kernel * scores[None], x_heads, precision=exact_precision)
    from_state = jnp.einsum("tn,hpn->thp", c_rows, state_in, precision=exact_precision)
    from_state = from_state * jnp.exp(running).T[:, :, None]
    outputs = inner + from_state + skip_gain[None, :, None] * x_heads
    retained, own_state = span_state(x_rows, b_rows, log_decay)
    state_out = retained[:, None, None] * state_in + own_state
    return (outputs.reshape(length, -1), state_out)


def boundary_grad(c_rows, log_decay, g_rows):
    length = g_rows.shape[0]
    heads = log_decay.shape[0]
    g_heads = g_rows.reshape(length, heads, -1)
    running = jnp.cumsum(log_decay, axis=1)
    return jnp.einsum(
        "thp,tn->hpn", g_heads * jnp.exp(running).T[:, :, None], c_rows, precision=exact_precision
    )


def combine_states(earlier, later):
    return (earlier[0] * later[0], later[0][:, None, None] * earlier[1] + later[1])


def local(inputs, w_in, b_rows, c_rows, log_decay, skip_gain, grad_out):
    weight = lax.all_gather(w_in, "ctx", axis=0, tiled=True)
    x_summed = jnp.dot(
        lax.all_gather(inputs, "head", axis=1, tiled=True),
        weight,
        preferred_element_type=jnp.float32,
    )
    x_rows = x_summed.astype(jnp.bfloat16)
    x_float = lax.optimization_barrier(x_rows).astype(jnp.float32)
    b_float = b_rows.astype(jnp.float32)
    c_float = c_rows.astype(jnp.float32)
    g_float = grad_out.astype(jnp.float32)
    heads = log_decay.shape[0]
    x_parts = [x_float[index * SPAN : (index + 1) * SPAN] for index in range(SPANS_DEV)]
    b_parts = [b_float[index * SPAN : (index + 1) * SPAN] for index in range(SPANS_DEV)]
    c_parts = [c_float[index * SPAN : (index + 1) * SPAN] for index in range(SPANS_DEV)]
    g_parts = [g_float[index * SPAN : (index + 1) * SPAN] for index in range(SPANS_DEV)]
    d_parts = [log_decay[:, index * SPAN : (index + 1) * SPAN] for index in range(SPANS_DEV)]
    span_states = [
        span_state(x_parts[index], b_parts[index], d_parts[index]) for index in range(SPANS_DEV)
    ]
    span_grads = [
        boundary_grad(c_parts[index], d_parts[index], g_parts[index]) for index in range(SPANS_DEV)
    ]
    forward_total = span_states[0]
    index = 1
    forward_total = combine_states(forward_total, span_states[index])
    backward_total = (span_states[SPANS_DEV - 1][0], span_grads[SPANS_DEV - 1])
    index = 0
    backward_total = combine_states(backward_total, (span_states[index][0], span_grads[index]))
    identity = (jnp.ones((heads,), jnp.float32), jnp.zeros(forward_total[1].shape, jnp.float32))
    device_state_in = entering(forward_total, "ctx", combine_states, identity, False)[1]
    device_grad_out = entering(backward_total, "ctx", combine_states, identity, True)[1]
    states_in = [device_state_in]
    index = 1
    previous = span_states[index - 1]
    states_in.append(previous[0][:, None, None] * states_in[index - 1] + previous[1])
    grads_out = [device_grad_out]
    index = 1
    grads_out.insert(0, span_grads[index] + span_states[index][0][:, None, None] * grads_out[0])
    grad_x_list = []
    grad_b_list = []
    grad_c_list = []
    grad_d_list = []
    for index in range(SPANS_DEV):
        state_here = states_in[index]

        def local_forward(x_value, b_value, c_value, d_value):
            return span_forward(x_value, b_value, c_value, d_value, state_here, skip_gain)

        _, pullback = jax.vjp(
            local_forward, x_parts[index], b_parts[index], c_parts[index], d_parts[index]
        )
        grad_x_part, grad_b_part, grad_c_part, grad_d_part = pullback(
            (g_parts[index], grads_out[index])
        )
        grad_x_list.append(grad_x_part)
        grad_b_list.append(grad_b_part)
        grad_c_list.append(grad_c_part)
        grad_d_list.append(grad_d_part)
    grad_x = jnp.concatenate(grad_x_list, axis=0)
    grad_b_local = jnp.concatenate(grad_b_list, axis=0)
    grad_c_local = jnp.concatenate(grad_c_list, axis=0)
    grad_log_decay = jnp.concatenate(grad_d_list, axis=1)
    grad_b, grad_c = (
        lax.psum(grad_b_local.astype(jnp.bfloat16), "head").astype(jnp.float32),
        lax.psum(grad_c_local.astype(jnp.bfloat16), "head").astype(jnp.float32),
    )
    grad_x_rows = grad_x.astype(jnp.bfloat16)
    partial_grads = lax.dot_general(
        grad_x_rows, weight, (((1,), (1,)), ((), ())), preferred_element_type=jnp.float32
    )
    grad_inputs = lax.psum_scatter(
        partial_grads.astype(jnp.bfloat16), "head", scatter_dimension=1, tiled=True
    )
    return (grad_inputs, grad_b, grad_c, grad_log_decay)


def solution(mesh):
    in_specs = (
        P("ctx", "head"),
        P("ctx", "head"),
        P("ctx", None),
        P("ctx", None),
        P("head", "ctx"),
        P("head"),
        P("ctx", "head"),
    )
    out_specs = (P("ctx", "head"), P("ctx", None), P("ctx", None), P("head", "ctx"))
    return jax.shard_map(local, mesh=mesh, in_specs=in_specs, out_specs=out_specs, check_vma=False)
```

profile of v0, /device:TPU:1, one launch (start us, length us, event | category | flops | bytes accessed | tf_op | source)
XLA Modules:
  0.0 934.2 jit_solution(13529698081639127813)
XLA Ops:
  11.4 1.2 fusion.127
  14.1 1.1 convolution_add_fusion.1
  15.3 1.3 dynamic-slice
  17.5 122.7 %all-reduce.4 = f32[512]{0:T(512)S(1)} all-reduce(f32[512]{0:T(512)S(1)} %dynamic-update-slice), channel_id=2, replica_groups=mesh['ctx'=64,'head'=8] {'ctx'}, use_global_device_ids=true, to_apply=%add.4 | all-reduce | flops 512 | bytes 4096
  141.5 55.0 %all-gather.8.cloned.1.call-done = bf16[4096,512]{1,0:T(8,128)(2,1)} async-done(((bf16[64,512]{1,0:T(8,128)(2,1)}), bf16[4096,512]{1,0:T(8,128)(2,1)}) %all-gather.8.cloned.1.call-update) | async-done | bytes 4194320 | tf_op jit(solution)/shard_map/all_gather | solution.py:76
  196.5 5.8 convolution_convert_fusion.1
  203.2 1.1 fusion.67
  204.2 191.7 %all-gather.12.cloned.1.call-done = f32[512,64,128]{2,1,0:T(8,128)} async-done(((f32[8,64,128]{2,1,0:T(8,128)}), f32[512,64,128]{2,1,0:T(8,128)}) %all-gather.12.cloned.1.call-update) | async-done | bytes 16777232 | tf_op jit(solution)/shard_map/all_gather | solution.py:17
  395.9 111.5 %while.26 = (s32[]{:T(128)}, f32[8,64,128]{2,1,0:T(8,128)S(1)}, s32[]{:T(128)}, f32[64,8]{1,0:T(8,128)}, f32[64,8,64,128]{3,2,1,0:T(8,128)}, /*index=5*/s32[]{:T(128)}, s32[]{:T(128)}, s32[]{:T(128)}, s32[]{:T(128)}) while((s32[]{:T(128)}, f32[8,64,128]{2,1,0:T(8,128)S(1)}, s32[]{:T(128)}, f32[64,8]{1,0:T(8,128)}, ...), condition=%wide.region_5.6_spmd, body=%wide.region_4.5_spmd.sunk | while | flops 131078 | bytes 786675 | solution.py:26
  396.6 1.1 bitcast_add_fusion.4
  400.2 1.1 bitcast_add_fusion.4
  401.9 1.1 bitcast_add_fusion.4
  403.7 1.1 bitcast_add_fusion.4
  405.5 1.1 bitcast_add_fusion.4
  407.2 1.1 bitcast_add_fusion.4
  410.8 1.1 bitcast_add_fusion.4
  412.5 1.1 bitcast_add_fusion.4
  414.3 1.1 bitcast_add_fusion.4
  416.1 1.1 bitcast_add_fusion.4
  419.6 1.1 bitcast_add_fusion.4
  421.4 1.1 bitcast_add_fusion.4
  423.1 1.1 bitcast_add_fusion.4
  424.9 1.1 bitcast_add_fusion.4
  426.7 1.1 bitcast_add_fusion.4
  428.5 1.1 bitcast_add_fusion.4
  430.2 1.1 bitcast_add_fusion.4
  433.8 1.1 bitcast_add_fusion.4
  507.5 2.1 multiply_reduce_fusion
  510.2 1.3 fusion.120
  512.1 2.1 convolution_add_fusion
  515.0 1.1 copy.73
  516.1 1.8 copy.70
  518.6 1.7 fusion.93
  520.3 1.7 fusion.98
  522.8 1.1 copy.78
  525.7 4.3 fusion.25
  531.3 2.5 fusion.40
  533.8 162.6 %all-gather.14.cloned.1.call-done = f32[512,64,128]{2,1,0:T(8,128)} async-done(((f32[8,64,128]{2,1,0:T(8,128)}), f32[512,64,128]{2,1,0:T(8,128)}) %all-gather.14.cloned.1.call-update) | async-done | bytes 16777232 | tf_op jit(solution)/shard_map/all_gather | solution.py:17
  702.3 1.8 fusion.43
  705.1 6.5 convolution_convert_fusion
  713.8 2.5 reduce-window.46
  716.4 2.5 reduce-window.50
  719.0 2.5 reduce-window.54
  721.7 2.5 reduce-window.56
  725.0 154.8 %all-reduce.8.cloned.1.call-done = (bf16[512,128]{1,0:T(8,128)(2,1)}, bf16[512,128]{1,0:T(8,128)(2,1)}) async-done(((bf16[512,128]{1,0:T(8,128)(2,1)}, bf16[512,128]{1,0:T(8,128)(2,1)}), (bf16[512,128]{1,0:T(8,128)(2,1)}, bf16[512,128]{1,0:T(8,128)(2,1)})) %all-reduce.8.cloned.1.call-update) | async-done | bytes 262160 | tf_op jit(solution)/shard_map/psum | solution.py:140
  879.8 1.6 convert_element_type.27
  881.4 1.6 convert_element_type.28
  883.1 44.3 %reduce-scatter.2.cloned.1.call-done = bf16[512,512]{1,0:T(8,128)(2,1)} async-done(((bf16[512,4096]{1,0:T(8,128)(2,1)}), bf16[512,512]{1,0:T(8,128)(2,1)}) %reduce-scatter.2.cloned.1.call-update) | async-done | bytes 524304 | tf_op jit(solution)/shard_map/reduce_scatter | solution.py:147
  (269 shorter events, 115.4 us)
Async XLA Ops:
  7.2 134.3 %all-gather.10.cloned.1.call-start = ((), (), s32[]{:S(2)}) async-start(), calls=%async_computation.3 | async-start | bytes 4718592 | tf_op jit(solution)/shard_map/all_gather | solution.py:78
  7.9 188.6 %all-gather.8.cloned.1.call-start = ((), (), s32[]{:S(2)}) async-start(), calls=%async_computation.1 | async-start | bytes 4259840 | tf_op jit(solution)/shard_map/all_gather | solution.py:76
  8.6 387.3 %all-gather.12.cloned.1.call-start = ((), (), s32[]{:S(2)}) async-start(), calls=%async_computation.4 | async-start | bytes 17039360 | tf_op jit(solution)/shard_map/all_gather | solution.py:17
  11.0 2.4 copy-start.14
  11.1 1.9 copy-start.16
  11.3 129.6 %copy-start.32 = (f32[8]{0:T(128)}, f32[8]{0:T(128)S(1)}, u32[]{:S(2)}) copy-start(f32[8]{0:T(128)S(1)} %get-tuple-element.143) | copy-start | bytes 100
  11.3 130.1 %copy-start.26 = (f32[8]{0:T(128)}, f32[8]{0:T(128)S(1)}, u32[]{:S(2)}) copy-start(f32[8]{0:T(128)S(1)} %get-tuple-element.145) | copy-start | bytes 100
  11.4 2.1 copy-start.34
  11.4 1.6 copy-start.4
  13.4 0.7 copy-start.1
  15.2 681.1 %all-gather.14.cloned.1.call-start = ((), (), s32[]{:S(2)}) async-start(), calls=%async_computation.5 | async-start | bytes 17039360 | tf_op jit(solution)/shard_map/all_gather | solution.py:17
  141.5 61.3 %copy-start.20 = (f32[256,8]{0,1:T(8,128)}, f32[256,8]{0,1:T(8,128)S(1)}, u32[]{:S(2)}) copy-start(f32[256,8]{0,1:T(8,128)S(1)} %fusion.115) | copy-start | bytes 24580
  202.3 0.9 copy-start.5
  507.5 6.7 copy-start
  509.6 0.6 copy-start.22
  511.5 0.6 copy-start.18
  514.2 365.6 %all-reduce.8.cloned.1.call-start = ((), (), s32[]{:S(2)}) async-start(), calls=%async_computation.6 | async-start | bytes 524288 | tf_op jit(solution)/shard_map/psum | solution.py:140
  524.7 0.9 copy-start.13
  525.6 4.3 copy-start.19
  525.6 5.6 copy-start.9
  525.7 5.6 copy-start.11
  525.7 5.6 copy-start.24
  525.7 5.6 copy-start.38
  530.0 3.8 copy-start.7
  696.4 1.0 copy-start.2
  696.4 1.0 copy-start.3
  696.4 1.0 copy-start.35
  696.4 1.0 copy-start.36
  696.4 1.3 copy-start.6
  696.6 1.5 copy-start.21
  696.7 2.5 copy-start.15
  697.4 2.7 copy-start.17
  697.7 3.5 copy-start.8
  698.1 4.1 copy-start.10
  698.1 4.1 copy-start.12
  698.1 4.1 copy-start.25
  702.3 2.8 copy-start.39
  704.8 222.5 %reduce-scatter.2.cloned.1.call-start = ((), (), s32[]{:S(2)}) async-start(), calls=%async_computation.2 | async-start | bytes 4718592 | tf_op jit(solution)/shard_map/reduce_scatter | solution.py:147
  711.6 0.6 copy-start.37
  711.6 0.7 copy-start.27
  711.6 2.1 copy-start.23
  711.6 2.1 copy-start.28
  711.6 2.1 copy-start.29
  711.6 2.1 copy-start.30
  711.6 2.1 copy-start.31
  711.6 2.1 copy-start.33
Sparse Core Ops, SparseCore 0:
  10.1 45.5 all-gather.9
  58.7 137.7 all-gather.7
  200.0 195.8 all-gather.11
  514.3 182.0 all-gather.13
  704.9 174.8 all-reduce.7
  883.3 43.9 reduce-scatter.1
where the time goes:
time: 940 us; the launch traced here: 934 us
  waiting for transfers between devices  610 us (65%)
  blocking collectives  123 us (13%)
  other arithmetic  85.5 us (9%)
  local copies, waits for them, and re-layouts  60.4 us (6%)
  matrix products  37.9 us (4%)
  between operations  15.4 us (2%)
    all_gather x2, waiting for transfers between devices, entering(): gathered = jax.tree.map(lambda a: lax.all_gather(a, axis), part)  354 us
    psum x1, waiting for transfers between devices, local(): lax.psum(grad_b_local.astype(jnp.bfloat16), 'head').astype(jnp.float32)  155 us
    unnamed x1, blocking collectives  123 us
    add x63, other arithmetic, combine_states(): later[0][:, None, None] * earlier[1] + later[1]  66.3 us
    all_gather x1, waiting for transfers between devices, local(): weight = lax.all_gather(w_in, 'ctx', axis=0, tiled=True)  55 us
    reduce_scatter x1, waiting for transfers between devices, local(): lax.psum_scatter(partial_grads.astype(jnp.bfloat16), 'head', scatter_dime...  44.3 us
    mul x63, local copies, waits for them, and re-layouts, combine_states(): later[0][:, None, None] * earlier[1] + later[1]  43.3 us
  transfers between devices with their start and end apart: 6, of which 5 were waited for; matrix products, arithmetic and copies ran while one was open for 6% of the time, Pallas kernels for 0%

commit v1 on v0

v1 whole, which is shorter than its diff:
```python
import jax
import jax.numpy as jnp
from jax import lax
from jax.experimental import pallas as pl
from jax.experimental.pallas import tpu as pltpu
from jax.sharding import PartitionSpec as P

MESH = pl.DeviceIdType.MESH
BF = jnp.bfloat16
F32 = jnp.float32
EXACT = lax.Precision.HIGHEST
NX, NY, NZ = 4, 4, 16
SPAN = 256
T = 512
CA = 256
CB = 512 - CA
NEG = -1e30


def mm(a, b, precision=None):
    return lax.dot_general(a, b, (((1,), (0,)), ((), ())), precision=precision, preferred_element_type=F32)


def mm_nt(a, b, precision=None):
    return lax.dot_general(a, b, (((1,), (1,)), ((), ())), precision=precision, preferred_element_type=F32)


def mm_tn(a, b):
    return lax.dot_general(a, b, (((0,), (0,)), ((), ())), preferred_element_type=F32)


def iota(shape, dim):
    return lax.broadcasted_iota(jnp.int32, shape, dim)


N_SEND = 240
N_RECV = 264


def kernel(
    inp_ref, w_ref, b_ref, c_ref, ld_ref, sk_ref, g_ref,
    gi_ref, gb_ref, gc_ref, gld_ref,
    wbuf, inpb, pbuf, sibr, yfar, ynear, lt_ref, mt_ref, gxf, gx, te_ref, v_ref, xacc, x_ref, ex_ref,
    rr_ref, rc_ref, a_ref, adev, ax_ref, az_ref,
    gst, est, qs, ss, sx_ref, xr, tz, zr, zo, zp, bo_ref, br_ref,
    dmt, drow, dcol, pr, prr, pfin, pfull,
    send_sem, recv_sem,
):
    ctx = lax.axis_index("ctx")
    head = lax.axis_index("head")
    z, x = ctx // NX, ctx % NX
    y, c = head // 2, head % 2

    def at_x(d):
        return (z * NX + (x + d) % NX, head)

    def at_z(d):
        return (((z + d) % NZ) * NX + x, head)

    def at_y(d):
        return (ctx, ((y + d) % NY) * 2 + c)

    sib = (ctx, y * 2 + (1 - c))

    def at_head(d):
        return (ctx, (head + d) % 8)

    counts = {"s": 0, "r": 0}
    sent = []

    def recv_slots(n):
        base = counts["r"]
        counts["r"] += n
        return base

    def copy(src, dst, slot, device):
        k = counts["s"]
        counts["s"] += 1
        d = pltpu.make_async_remote_copy(
            src_ref=src, dst_ref=dst, send_sem=send_sem.at[k], recv_sem=recv_sem.at[slot],
            device_id=device, device_id_type=MESH,
        )
        d.start()
        sent.append(d)

    def arrived(dst, slot):
        pltpu.make_async_remote_copy(
            src_ref=dst, dst_ref=dst, send_sem=send_sem.at[0], recv_sem=recv_sem.at[slot],
            device_id=sib, device_id_type=MESH,
        ).wait_recv()

    barrier = pltpu.get_barrier_semaphore()
    peers = [at_x(d) for d in range(1, NX)] + [at_z(d) for d in range(1, NZ)] + [at_head(d) for d in range(1, 8)]
    for peer in peers:
        pl.semaphore_signal(barrier, inc=1, device_id=peer, device_id_type=MESH)
    pl.semaphore_wait(barrier, len(peers))

    def wrows(zz, xx):
        return pl.ds(pl.multiple_of((zz * NX + xx) * 64, 64), 64)

    def wgroup(zz):
        return pl.ds(pl.multiple_of(zz * 256, 256), 256)

    colsA, colsB = pl.ds(0, CA), pl.ds(CA, CB)
    HB = 128 * ((CB // 2 + 127) // 128)
    colsB1, colsB2 = pl.ds(CA, HB), pl.ds(CA + HB, CB - HB)
    w0 = recv_slots(4)
    for d in (1, 3, 2):
        copy(w_ref, wbuf.at[wrows(z, x), :], w0 + d, at_x(d))
    bR, bL, aR, aL = recv_slots(9), recv_slots(9), recv_slots(9), recv_slots(9)
    copy(w_ref.at[:, colsB], wbuf.at[wrows(z, x), colsB], bR + 1, at_z(1))
    copy(w_ref.at[:, colsB], wbuf.at[wrows(z, x), colsB], bL + 1, at_z(NZ - 1))

    half = (pl.ds(0, 256), pl.ds(256, 256))
    iR, iL, iF, iS = recv_slots(2), recv_slots(2), recv_slots(2), recv_slots(8)

    def ihead(d):
        return ((y + d) % NY) * 2 + c

    copy(inp_ref.at[:, half[0]], inpb.at[head, :, half[0]], iR + 0, at_y(1))
    copy(inp_ref.at[:, half[1]], inpb.at[head, :, half[1]], iL + 1, at_y(3))
    copy(inp_ref.at[:, half[1]], inpb.at[head, :, half[1]], iR + 1, at_y(1))
    copy(inp_ref.at[:, half[0]], inpb.at[head, :, half[0]], iL + 0, at_y(3))
    copy(inp_ref, inpb.at[head], iS + 0, sib)

    wbuf[wrows(z, x), :] = w_ref[...]
    inpb[head] = inp_ref[...]

    def input_pass(part):
        left, right, far = ihead(3), ihead(1), ihead(2)
        if part == 0:
            arrived(inpb.at[left, :, half[0]], iR + 0)
            copy(inpb.at[left, :, half[0]], inpb.at[left, :, half[0]], iF + 0, at_y(1))
            arrived(inpb.at[right, :, half[1]], iL + 1)
            copy(inpb.at[right, :, half[1]], inpb.at[right, :, half[1]], iF + 1, at_y(3))
            copy(inpb.at[left, :, half[0]], inpb.at[left, :, half[0]], iS + 1, sib)
            copy(inpb.at[right, :, half[1]], inpb.at[right, :, half[1]], iS + 2, sib)
        if part == 1:
            arrived(inpb.at[left, :, half[1]], iR + 1)
            copy(inpb.at[left, :, half[1]], inpb.at[left, :, half[1]], iS + 3, sib)
            arrived(inpb.at[right, :, half[0]], iL + 0)
            copy(inpb.at[right, :, half[0]], inpb.at[right, :, half[0]], iS + 4, sib)
        if part == 2:
            for k in (0, 1):
                arrived(inpb.at[far, :, half[k]], iF + k)
                copy(inpb.at[far, :, half[k]], inpb.at[far, :, half[k]], iS + 5 + k, sib)
        if part == 3:
            def other(d):
                return ((y + d) % NY) * 2 + (1 - c)
            arrived(inpb.at[other(0)], iS + 0)
            arrived(inpb.at[other(3), :, half[0]], iS + 1)
            arrived(inpb.at[other(1), :, half[1]], iS + 2)
            arrived(inpb.at[other(3), :, half[1]], iS + 3)
            arrived(inpb.at[other(1), :, half[0]], iS + 4)
            for k in (0, 1):
                arrived(inpb.at[other(2), :, half[k]], iS + 5 + k)

    def w_start():
        for d in (1, 2, 3):
            arrived(wbuf.at[wrows(z, (x + NX - d) % NX), :], w0 + d)
        copy(wbuf.at[wgroup(z), colsA], wbuf.at[wgroup(z), colsA], aR + 1, at_z(1))
        copy(wbuf.at[wgroup(z), colsA], wbuf.at[wgroup(z), colsA], aL + 1, at_z(NZ - 1))

    xslots = {}

    def w_across(key, zz):
        base = recv_slots(4)
        xslots[key] = base
        blk = wbuf.at[wrows(zz, x), colsB]
        copy(blk, blk, base + 0, at_x(1))
        copy(blk, blk, base + 1, at_x(3))

    def w_across2(key, zz):
        base = xslots[key]
        left, right = (x + 3) % NX, (x + 1) % NX
        arrived(wbuf.at[wrows(zz, left), colsB], base + 0)
        blk = wbuf.at[wrows(zz, left), colsB1]
        copy(blk, blk, base + 2, at_x(1))
        arrived(wbuf.at[wrows(zz, right), colsB], base + 1)
        blk = wbuf.at[wrows(zz, right), colsB2]
        copy(blk, blk, base + 3, at_x(3))

    def w_step(s):
        zr_, zl_ = (z + NZ - s) % NZ, (z + s) % NZ
        if s <= 8:
            blk = wbuf.at[wgroup(zr_), colsA]
            arrived(blk, aR + s)
            if s < 8:
                copy(blk, blk, aR + s + 1, at_z(1))
        if s <= 7:
            blk = wbuf.at[wgroup(zl_), colsA]
            arrived(blk, aL + s)
            if s < 7:
                copy(blk, blk, aL + s + 1, at_z(NZ - 1))
        if s <= 7:
            blk = wbuf.at[wrows(zr_, x), colsB]
            arrived(blk, bR + s)
            if s < 7:
                copy(blk, blk, bR + s + 1, at_z(1))
            w_across(("R", s), zr_)
        if s <= 8:
            blk = wbuf.at[wrows(zl_, x), colsB]
            arrived(blk, bL + s)
            if s < 8:
                copy(blk, blk, bL + s + 1, at_z(NZ - 1))
            w_across(("L", s), zl_)
        if s >= 2:
            w_late(s - 1)

    def w_late(s):
        if s <= 7:
            w_across2(("R", s), (z + NZ - s) % NZ)
        if s <= 8:
            w_across2(("L", s), (z + s) % NZ)

    def w_end():
        w_late(8)
        far = (x + 2) % NX
        for (side, s), base in xslots.items():
            zz = (z + NZ - s) % NZ if side == "R" else (z + s) % NZ
            arrived(wbuf.at[wrows(zz, far), colsB1], base + 2)
            arrived(wbuf.at[wrows(zz, far), colsB2], base + 3)

    lane = iota((SPAN, 128), 1)
    low = lane < 64
    lowrow = iota((1, 128), 1) < 64
    ti, tj = iota((SPAN, SPAN), 0), iota((SPAN, SPAN), 1)
    upto = ti <= tj

    def pair(col, i):
        return jnp.where(low, col[:, 2 * i:2 * i + 1], col[:, 2 * i + 1:2 * i + 2])

    def pair_row(row, i):
        return jnp.where(lowrow, row[:, 2 * i:2 * i + 1], row[:, 2 * i + 1:2 * i + 2])

    def first(sp):
        rows = pl.ds(sp * SPAN, SPAN)
        rr = mm(ld_ref[:, rows], upto.astype(F32), EXACT)
        rc = jnp.concatenate([rr, jnp.zeros((120, SPAN), F32)], 0).T
        rr_ref[sp] = rr
        rc_ref[sp] = rc
        last = rc[SPAN - 1:SPAN, :]
        ec, tc, al = jnp.exp(rc), jnp.exp(last - rc), jnp.exp(last)
        ct = c_ref[rows, :].T
        for i in range(4):
            cols = pl.ds(i * 128, 128)
            v = (g_ref[rows, cols].astype(F32) * pair(ec, i)).astype(BF)
            v_ref[rows, cols] = v
            te_ref[rows, cols] = pair(tc, i)
            a_ref[sp, i] = jnp.broadcast_to(pair_row(al, i), (8, 128))
            gst[sp, i] = mm(ct, v)
        mt_ref[sp] = mm_nt(b_ref[rows, :], c_ref[rows, :])

    def unit1(sp, i):
        rows, cols = pl.ds(sp * SPAN, SPAN), pl.ds(i * 128, 128)
        g2 = g_ref[rows, cols]
        mt = mt_ref[sp]
        parts = []
        for k in (0, 1):
            h = 2 * i + k
            diff = rr_ref[sp, h:h + 1, :] - rc_ref[sp, :, h:h + 1]
            lt = jnp.exp(jnp.where(upto, diff, NEG))
            lt_ref[sp * 8 + h] = lt
            parts.append(mm((lt * mt).astype(BF), g2))
        skip = jnp.where(lowrow, sk_ref[2 * i], sk_ref[2 * i + 1])
        gxf[rows, cols] = jnp.where(low, parts[0], parts[1]) + skip * g2.astype(F32)

    def scan_x_send(which, state):
        base = recv_slots(4)
        for i in range(4):
            sx_ref[which, i] = state(i).astype(BF)
        for d in (1, 3, 2):
            to = (x + d) % NX
            copy(sx_ref.at[which, to], xr.at[which, x], base + d, at_x(d))
        xr[which, x] = sx_ref[which, x]
        return base

    def scan_x_wait(which, base):
        for d in (1, 2, 3):
            arrived(xr.at[which, (x + NX - d) % NX], base + d)

    def scan_z_send(which):
        base = recv_slots(16)
        for d in range(1, NZ):
            to = (z + d) % NZ
            copy(tz.at[which, to], zr.at[which, z], base + d, at_z(d))
        zr[which, z] = tz[which, z]
        return base

    def scan_z_wait(which, base):
        for d in range(1, NZ):
            arrived(zr.at[which, (z + NZ - d) % NZ], base + d)

    def scan_z_back(which):
        base = recv_slots(16)
        for d in range(1, NZ):
            to = (z + d) % NZ
            copy(zo.at[which, to], zp.at[which, z], base + d, at_z(d))
        zp[which, z] = zo[which, z]
        return base

    def scan_z_back_wait(which, base):
        for d in range(1, NZ):
            arrived(zp.at[which, (z + NZ - d) % NZ], base + d)

    def scan_x_back(which):
        base = recv_slots(4)
        for d in (1, 3, 2):
            to = (x + d) % NX
            copy(bo_ref.at[which, to], br_ref.at[which, x], base + d, at_x(d))
        br_ref[which, x] = bo_ref[which, x]
        return base

    def scan_x_back_wait(which, base):
        for d in (1, 2, 3):
            arrived(br_ref.at[which, (x + NX - d) % NX], base + d)

    marks = {}

    def ret_x():
        base = recv_slots(4)
        for i in range(4):
            adev[i] = a_ref[0, i] * a_ref[1, i]
        for d in (1, 3, 2):
            to = (x + d) % NX
            copy(adev.at[to], ax_ref.at[x], base + d, at_x(d))
        ax_ref[x] = adev[x]
        marks["ax"] = base

    def ret_z():
        for d in (1, 2, 3):
            arrived(ax_ref.at[(x + NX - d) % NX], marks["ax"] + d)
        base = recv_slots(16)
        adev[4] = ax_ref[0] * ax_ref[1] * ax_ref[2] * ax_ref[3]
        for d in range(1, NZ):
            copy(adev.at[4], az_ref.at[z], base + d, at_z(d))
        az_ref[z] = adev[4]
        marks["az"] = base

    def ret_wait():
        for d in range(1, NZ):
            arrived(az_ref.at[(z + NZ - d) % NZ], marks["az"] + d)

    def ret(k):
        return ax_ref[k][0:1, :]

    def put_total(which, total):
        for k in range(NZ):
            tz[which, k] = total[8 * k:8 * k + 8, :]

    def bscan(part):
        if part == 0:
            marks["b0"] = scan_x_send(0, lambda i: gst[0, i] + a_ref[0, i][0:1, :] * gst[1, i])
        if part == 1:
            scan_x_wait(0, marks["b0"])
            total = xr[0, 3].astype(F32)
            for k in (2, 1, 0):
                total = xr[0, k].astype(F32) + ret(k) * total
            put_total(0, total)
            marks["b1"] = scan_z_send(0)
        if part == 2:
            ret_wait()
            scan_z_wait(0, marks["b1"])
            q = jnp.zeros((8, 128), F32)
            for k in range(NZ - 1, -1, -1):
                zo[0, k] = q
                q = zr[0, k] + az_ref[k] * q
            marks["b2"] = scan_z_back(0)
        if part == 3:
            scan_z_back_wait(0, marks["b2"])
            q = jnp.concatenate([zp[0, k] for k in range(NZ)], 0)
            for k in (3, 2, 1, 0):
                bo_ref[0, k] = q.astype(BF)
                if k:
                    q = xr[0, k].astype(F32) + ret(k) * q
            marks["b3"] = scan_x_back(0)
        if part == 4:
            scan_x_back_wait(0, marks["b3"])
            for i in range(4):
                cols = pl.ds(i * 128, 128)
                q = br_ref[0, i]
                qs[1, :, cols] = q
                qs[0, :, cols] = (gst[1, i] + a_ref[1, i][0:1, :] * q.astype(F32)).astype(BF)

    def fscan(part):
        if part == 0:
            marks["f0"] = scan_x_send(1, lambda i: a_ref[1, i][0:1, :] * est[0, i] + est[1, i])
        if part == 1:
            scan_x_wait(1, marks["f0"])
            total = xr[1, 0].astype(F32)
            for k in (1, 2, 3):
                total = xr[1, k].astype(F32) + ret(k) * total
            put_total(1, total)
            marks["f1"] = scan_z_send(1)
        if part == 2:
            scan_z_wait(1, marks["f1"])
            s = jnp.zeros((8, 128), F32)
            for k in range(NZ):
                zo[1, k] = s
                s = zr[1, k] + az_ref[k] * s
            marks["f2"] = scan_z_back(1)
        if part == 3:
            scan_z_back_wait(1, marks["f2"])
            s = jnp.concatenate([zp[1, k] for k in range(NZ)], 0)
            for k in range(NX):
                bo_ref[1, k] = s.astype(BF)
                if k < NX - 1:
                    s = xr[1, k].astype(F32) + ret(k) * s
            marks["f3"] = scan_x_back(1)
        if part == 4:
            scan_x_back_wait(1, marks["f3"])
            for i in range(4):
                cols = pl.ds(i * 128, 128)
                s = br_ref[1, i]
                ss[0, :, cols] = s
                ss[1, :, cols] = (a_ref[0, i][0:1, :] * s.astype(F32) + est[0, i]).astype(BF)

    def finish_gx(sp):
        rows = pl.ds(sp * SPAN, SPAN)
        gx[rows, :] = (gxf[rows, :] + te_ref[rows, :] * mm(b_ref[rows, :], qs[sp])).astype(BF)

    def project():
        xacc[...] = jnp.zeros_like(xacc)

        def one(j, carry):
            xacc[...] += mm(inpb[j], wbuf[pl.ds(pl.multiple_of(j * 512, 512), 512), :])
            return carry

        lax.fori_loop(0, 8, one, 0)
        xb = xacc[...].astype(BF)
        x_ref[...] = xb
        ex_ref[...] = (te_ref[...] * xb.astype(F32)).astype(BF)
        for sp in range(2):
            rows = pl.ds(sp * SPAN, SPAN)
            bt = b_ref[rows, :].T
            for i in range(4):
                est[sp, i] = mm(bt, ex_ref[rows, pl.ds(i * 128, 128)])

    rS = recv_slots(4)

    def wblock(j):
        return wbuf[pl.ds(pl.multiple_of(j * 512, 512), 512), :]

    def rs_sib():
        for d in (2, 1, 3, 0):
            j = ((y + d) % NY) * 2 + (1 - c)
            pbuf[j] = mm_nt(gx[...], wblock(j)).astype(BF)
            copy(pbuf.at[j], sibr.at[(y + d) % NY], rS + d, sib)

    rF, rN = recv_slots(2), recv_slots(4)

    def rs_own(d):
        yy = (y + d) % NY
        j = yy * 2 + c
        own = mm_nt(gx[...], wblock(j))
        arrived(sibr.at[yy], rS + d)
        pbuf[j] = (own + sibr[yy].astype(F32)).astype(BF)
        if d == 2:
            copy(pbuf.at[j, :, half[1]], yfar.at[:, half[1]], rF + 1, at_y(1))
            copy(pbuf.at[j, :, half[0]], yfar.at[:, half[0]], rF + 0, at_y(3))
        if d == 1:
            copy(pbuf.at[j, :, half[0]], ynear.at[0, :, half[0]], rN + 0, at_y(1))
        if d == 3:
            copy(pbuf.at[j, :, half[1]], ynear.at[1, :, half[1]], rN + 1, at_y(3))

    def rs_pass():
        j = ((y + 1) % NY) * 2 + c
        arrived(yfar.at[:, half[1]], rF + 1)
        pbuf[j, :, 256:512] = (pbuf[j, :, 256:512].astype(F32) + yfar[:, 256:512].astype(F32)).astype(BF)
        copy(pbuf.at[j, :, half[1]], ynear.at[0, :, half[1]], rN + 2, at_y(1))
        j = ((y + 3) % NY) * 2 + c
        arrived(yfar.at[:, half[0]], rF + 0)
        pbuf[j, :, 0:256] = (pbuf[j, :, 0:256].astype(F32) + yfar[:, 0:256].astype(F32)).astype(BF)
        copy(pbuf.at[j, :, half[0]], ynear.at[1, :, half[0]], rN + 3, at_y(3))

    def rs_end():
        arrived(ynear.at[0, :, half[0]], rN + 0)
        arrived(ynear.at[1, :, half[1]], rN + 1)
        arrived(ynear.at[0, :, half[1]], rN + 2)
        arrived(ynear.at[1, :, half[0]], rN + 3)
        gi_ref[...] = (
            pbuf[head].astype(F32) + ynear[0].astype(F32) + ynear[1].astype(F32)
        ).astype(BF)

    def unit2(sp):
        rows = pl.ds(sp * SPAN, SPAN)
        dmt[sp] = jnp.zeros((SPAN, SPAN), F32)
        dcol[sp] = jnp.zeros((SPAN, 128), F32)

        def one(i, carry):
            cols = pl.ds(pl.multiple_of(i * 128, 128), 128)
            g2, x2 = g_ref[rows, cols], x_ref[rows, cols]
            mt = mt_ref[sp]
            for k in (0, 1):
                h = 2 * i + k
                xm = jnp.where(low if k == 0 else jnp.logical_not(low), x2, jnp.zeros_like(x2))
                p = mm_nt(xm, g2) * lt_ref[sp * 8 + h]
                dmt[sp] += p
                wm = p * mt
                drow[sp, pl.ds(h, 1), :] = jnp.sum(wm, axis=0, keepdims=True)
                dcol[sp] += jnp.where(lane == h, jnp.sum(wm, axis=1, keepdims=True), 0.0)
            return carry

        lax.fori_loop(0, 4, one, 0)

    ind = (iota((8, 512), 1) // 64 == iota((8, 512), 0)).astype(BF)

    def head_sums(value):
        hi = value.astype(BF)
        lo = (value - hi.astype(F32)).astype(BF)
        return mm_nt(ind, hi) + mm_nt(ind, lo)

    def grad_b_part(sp):
        rows = pl.ds(sp * SPAN, SPAN)
        pr[0, rows, :] = (mm(dmt[sp].astype(BF), c_ref[rows, :]) + mm_nt(ex_ref[rows, :], qs[sp])).astype(BF)

    def grad_c_part(sp):
        rows = pl.ds(sp * SPAN, SPAN)
        pr[1, rows, :] = (
            mm_tn(dmt[sp].astype(BF), b_ref[rows, :]) + mm_nt(v_ref[rows, :], ss[sp])
        ).astype(BF)

    def decay_part(sp):
        rows = pl.ds(sp * SPAN, SPAN)
        u = mm(c_ref[rows, :], ss[sp])
        arow = jnp.concatenate([a_ref[sp, i][0:1, :] for i in range(4)], 1)
        cross = jnp.sum(qs[sp].astype(F32) * ss[sp].astype(F32), axis=0, keepdims=True) * arow
        is_last = iota((SPAN, 512), 0) == SPAN - 1
        vv = v_ref[rows, :].astype(F32) * u + jnp.where(is_last, cross, 0.0)
        tt = te_ref[rows, :] * x_ref[rows, :].astype(F32) * mm(b_ref[rows, :], qs[sp])
        dr = head_sums(vv) + drow[sp] - dcol[sp].T[0:8, :]
        gld_ref[:, rows] = mm(dr, (ti >= tj).astype(F32), EXACT) + mm(head_sums(tt), (ti < tj).astype(F32), EXACT)

    def mine(k):
        return pl.ds(pl.multiple_of(k * 64, 64), 64)

    def ps_send(which):
        base = recv_slots(8)
        for d in range(1, 8):
            to = (head + d) % 8
            copy(pr.at[which, mine(to), :], prr.at[which, head], base + d, at_head(d))
        prr[which, head] = pr[which, mine(head), :]
        return base

    def ps_sum(which, base):
        for d in range(1, 8):
            arrived(prr.at[which, (head + 8 - d) % 8], base + d)
        total = prr[which, 0].astype(F32)
        for k in range(1, 8):
            total = total + prr[which, k].astype(F32)
        pfin[which] = total.astype(BF)
        base = recv_slots(8)
        for d in range(1, 8):
            copy(pfin.at[which], pfull.at[which, mine(head), :], base + d, at_head(d))
        pfull[which, mine(head), :] = pfin[which]
        return base

    def ps_end(which, base, out):
        for d in range(1, 8):
            arrived(pfull.at[which, mine((head + 8 - d) % 8), :], base + d)
        out[...] = pfull[which].astype(F32)

    first(0)
    first(1)
    ret_x()
    bscan(0)
    w_start()
    ret_z()
    bscan(1)
    for s in range(1, 9):
        unit1((s - 1) // 4, (s - 1) % 4)
        w_step(s)
        if s == 1:
            bscan(2)
        if s == 2:
            bscan(3)
            input_pass(0)
        if s == 3:
            bscan(4)
            input_pass(1)
        if s == 5:
            input_pass(2)
    input_pass(3)
    finish_gx(0)
    finish_gx(1)
    w_end()
    project()
    fscan(0)
    rs_sib()
    fscan(1)
    rs_own(2)
    fscan(2)
    rs_own(1)
    rs_own(3)
    rs_own(0)
    fscan(3)
    unit2(0)
    rs_pass()
    unit2(1)
    grad_b_part(0)
    grad_b_part(1)
    pb = ps_send(0)
    fscan(4)
    grad_c_part(0)
    grad_c_part(1)
    pc = ps_send(1)
    pb = ps_sum(0, pb)
    decay_part(0)
    pc = ps_sum(1, pc)
    decay_part(1)
    ps_end(0, pb, gb_ref)
    ps_end(1, pc, gc_ref)
    rs_end()
    for d in sent:
        d.wait_send()
    assert counts["s"] <= N_SEND and counts["r"] <= N_RECV, counts


def local(inputs, w_in, b_rows, c_rows, log_decay, skip_gain, grad_out):
    vmem = pl.BlockSpec(memory_space=pltpu.VMEM)
    V = pltpu.VMEM
    return pl.pallas_call(
        kernel,
        out_shape=(
            jax.ShapeDtypeStruct((T, 512), BF),
            jax.ShapeDtypeStruct((T, 128), F32),
            jax.ShapeDtypeStruct((T, 128), F32),
            jax.ShapeDtypeStruct((8, T), F32),
        ),
        in_specs=[vmem] * 5 + [pl.BlockSpec(memory_space=pltpu.SMEM), vmem],
        out_specs=(vmem,) * 4,
        scratch_shapes=[
            V((4096, 512), BF),
            V((8, T, 512), BF),
            V((8, T, 512), BF),
            V((4, T, 512), BF),
            V((T, 512), BF),
            V((2, T, 512), BF),
            V((16, SPAN, SPAN), F32),
            V((2, SPAN, SPAN), F32),
            V((T, 512), F32),
            V((T, 512), BF),
            V((T, 512), F32),
            V((T, 512), BF),
            V((T, 512), F32),
            V((T, 512), BF),
            V((T, 512), BF),
            V((2, 8, SPAN), F32),
            V((2, SPAN, 128), F32),
            V((2, 4, 8, 128), F32),
            V((5, 8, 128), F32),
            V((4, 8, 128), F32),
            V((16, 8, 128), F32),
            V((2, 4, 128, 128), F32),
            V((2, 4, 128, 128), F32),
            V((2, 128, 512), BF),
            V((2, 128, 512), BF),
            V((2, 4, 128, 128), BF),
            V((2, 4, 128, 128), BF),
            V((2, 16, 8, 128), F32),
            V((2, 16, 8, 128), F32),
            V((2, 16, 8, 128), F32),
            V((2, 16, 8, 128), F32),
            V((2, 4, 128, 128), BF),
            V((2, 4, 128, 128), BF),
            V((2, SPAN, SPAN), F32),
            V((2, 8, SPAN), F32),
            V((2, SPAN, 128), F32),
            V((2, T, 128), BF),
            V((2, 8, 64, 128), BF),
            V((2, 64, 128), BF),
            V((2, T, 128), BF),
            pltpu.SemaphoreType.DMA((N_SEND,)),
            pltpu.SemaphoreType.DMA((N_RECV,)),
        ],
        compiler_params=pltpu.CompilerParams(
            collective_id=0, has_side_effects=True, vmem_limit_bytes=52 * 1024 * 1024
        ),
        cost_estimate=pl.CostEstimate(flops=8 * 10**9, bytes_accessed=4 * 10**6, transcendentals=2 * 10**6),
    )(inputs, w_in, b_rows, c_rows, log_decay, skip_gain, grad_out)


def solution(mesh):
    in_specs = (
        P("ctx", "head"),
        P("ctx", "head"),
        P("ctx", None),
        P("ctx", None),
        P("head", "ctx"),
        P("head"),
        P("ctx", "head"),
    )
    out_specs = (P("ctx", "head"), P("ctx", None), P("ctx", None), P("head", "ctx"))
    return jax.shard_map(local, mesh=mesh, in_specs=in_specs, out_specs=out_specs, check_vma=False)
```

time: 940 us -> 127 us (0.14)
  waiting for transfers between devices: 610 us -> 0 us
  blocking collectives: 123 us -> 0 us
  Pallas kernels: 0 us -> 118 us
  other arithmetic: 85.5 us -> 0 us
  local copies, waits for them, and re-layouts: 60.4 us -> 7.86 us
  matrix products: 37.9 us -> 0 us
  between operations: 15.4 us -> 0.66 us
    all_gather x4 -> x0, waiting for transfers between devices: 409 us -> none  [the longest x2 354 us: entering(): gathered = jax.tree.map(lambda a: lax.all_gather(a, axis), part)]
    psum x1 -> x0, waiting for transfers between devices: 155 us -> none  [local(): lax.psum(grad_b_local.astype(jnp.bfloat16), 'head').astype(jnp.float32)]
    unnamed x1 -> x0, blocking collectives: 123 us -> none
    pallas_call x0 -> x1, Pallas kernels: none -> 118 us  [local(): pl.pallas_call(kernel, out_shape=(jax.ShapeDtypeStruct((T, 512), BF), jax...]
    add x63 -> x0, other arithmetic: 66.3 us -> none  [combine_states(): later[0][:, None, None] * earlier[1] + later[1]]
    reduce_scatter x1 -> x0, waiting for transfers between devices: 44.3 us -> none  [local(): lax.psum_scatter(partial_grads.astype(jnp.bfloat16), 'head', scatter_dime...]
    mul x63 -> x0, local copies, waits for them, and re-layouts: 43.3 us -> none  [combine_states(): later[0][:, None, None] * earlier[1] + later[1]]
    dot_general x24 -> x0, matrix products: 37.9 us -> none  [the longest x4 9.02 us: span_forward(): jnp.einsum('hts,shp->thp', kernel * scores[None], x_heads, precision=exac...]
  transfers between devices with their start and end apart: 6 -> 0, of which waited for: 5 -> 0; matrix products, arithmetic and copies ran while one was open for 6% -> 0% of each run, Pallas kernels for 0% -> 0%
where the time goes in v1:
time: 127 us
  Pallas kernels  118 us (93%)
  local copies, waits for them, and re-layouts  7.86 us (6%)
    pallas_call x1, Pallas kernels, local(): pl.pallas_call(kernel, out_shape=(jax.ShapeDtypeStruct((T, 512), BF), jax...  118 us
    unnamed x16, local copies, waits for them, and re-layouts  7.86 us

profile of v1, /device:TPU:1, one launch (start us, length us, event | category | flops | bytes accessed | tf_op | source)
XLA Modules:
  0.0 126.9 jit_solution(13752436716343571199)
XLA Ops:
  0.6 0.0 copy-start
  0.6 1.0 copy-done
  1.7 0.0 copy-start.1
  1.7 0.9 copy-done.1
  2.6 0.0 copy-start.2
  2.6 0.9 copy-done.2
  3.5 0.0 copy-start.3
  3.5 0.8 copy-done.3
  4.3 0.0 copy-start.4
  4.3 0.7 copy-done.4
  5.0 0.0 copy-start.5
  5.0 0.7 copy-done.5
  5.7 118.3 %shard_map.102 = (bf16[512,512]{1,0:T(8,128)(2,1)S(1)}, f32[512,128]{1,0:T(8,128)S(1)}, f32[512,128]{1,0:T(8,128)S(1)}, f32[8,512]{1,0:T(8,128)S(1)}) custom-call(bf16[512,512]{1,0:T(8,128)(2,1)S(1)} %copy-done, bf16[64,512]{1,0:T(8,128)(2,1)S(1)} %copy-done.3, bf16[512,128]{1,0:T(8,128)(2,1)S(1)} %copy-done.1, bf16[512,128]{1,0:T(8,128)(2,1)S(1)} %copy-done.2, ...), custom_call_target="tpu_custom_call" | custom-call | flops 8000000000 | bytes 4000000 | tf_op jit(solution)/shard_map/pallas_call | solution.py:622
  124.1 0.8 copy.15
  124.8 0.7 copy.16
  125.6 0.7 copy.17
  126.3 0.6 copy.18
Async XLA Ops:
  0.6 1.0 copy-start
  1.7 0.9 copy-start.1
  2.6 0.9 copy-start.2
  3.5 0.8 copy-start.3
  4.3 0.7 copy-start.4
  5.0 0.7 copy-start.5

commit v2 on v1

--- a/solution.py
+++ b/solution.py
@@ -12,9 +12,9 @@
 NX, NY, NZ = 4, 4, 16
 SPAN = 256
 T = 512
-CA = 256
-CB = 512 - CA
 NEG = -1e30
+Q_FROM = 4
+FAR_FIRST = sorted(range(1, NZ), key=lambda d: -min(d, NZ - d))
 
 
 def mm(a, b, precision=None):
@@ -33,18 +33,19 @@
     return lax.broadcasted_iota(jnp.int32, shape, dim)
 
 
-N_SEND = 240
-N_RECV = 264
+N_SEND = 300
+N_RECV = 340
 
 
 def kernel(
-    inp_ref, w_ref, b_ref, c_ref, ld_ref, sk_ref, g_ref,
-    gi_ref, gb_ref, gc_ref, gld_ref,
+    inp_ref, w_ref, b_hbm, c_hbm, ld_hbm, sk_ref, g_hbm,
+    gi_hbm, gb_hbm, gc_hbm, gld_hbm,
+    b_ref, c_ref, ld_ref, g_ref, gi_ref, gb_ref, gc_ref, gld_ref,
     wbuf, inpb, pbuf, sibr, yfar, ynear, lt_ref, mt_ref, gxf, gx, te_ref, v_ref, xacc, x_ref, ex_ref,
     rr_ref, rc_ref, a_ref, adev, ax_ref, az_ref,
     gst, est, qs, ss, sx_ref, xr, tz, zr, zo, zp, bo_ref, br_ref,
     dmt, drow, dcol, pr, prr, pfin, pfull,
-    send_sem, recv_sem,
+    send_sem, recv_sem, load_sem,
 ):
     ctx = lax.axis_index("ctx")
     head = lax.axis_index("head")
@@ -89,27 +90,112 @@
             device_id=sib, device_id_type=MESH,
         ).wait_recv()
 
+    loads = []
+    for src, dst in ((ld_hbm, ld_ref), (c_hbm, c_ref), (g_hbm, g_ref), (b_hbm, b_ref)):
+        d = pltpu.make_async_copy(src, dst, load_sem.at[len(loads)])
+        d.start()
+        loads.append(d)
+
     barrier = pltpu.get_barrier_semaphore()
     peers = [at_x(d) for d in range(1, NX)] + [at_z(d) for d in range(1, NZ)] + [at_head(d) for d in range(1, 8)]
     for peer in peers:
         pl.semaphore_signal(barrier, inc=1, device_id=peer, device_id_type=MESH)
     pl.semaphore_wait(barrier, len(peers))
 
-    def wrows(zz, xx):
-        return pl.ds(pl.multiple_of((zz * NX + xx) * 64, 64), 64)
-
-    def wgroup(zz):
-        return pl.ds(pl.multiple_of(zz * 256, 256), 256)
-
-    colsA, colsB = pl.ds(0, CA), pl.ds(CA, CB)
-    HB = 128 * ((CB // 2 + 127) // 128)
-    colsB1, colsB2 = pl.ds(CA, HB), pl.ds(CA + HB, CB - HB)
-    w0 = recv_slots(4)
-    for d in (1, 3, 2):
-        copy(w_ref, wbuf.at[wrows(z, x), :], w0 + d, at_x(d))
-    bR, bL, aR, aL = recv_slots(9), recv_slots(9), recv_slots(9), recv_slots(9)
-    copy(w_ref.at[:, colsB], wbuf.at[wrows(z, x), colsB], bR + 1, at_z(1))
-    copy(w_ref.at[:, colsB], wbuf.at[wrows(z, x), colsB], bL + 1, at_z(NZ - 1))
+    every = slice(None)
+    pairs = (pl.ds(0, 2), pl.ds(2, 2))
+    P_ = [(two, every, pl.ds(0, 128)) for two in pairs]
+    Q_ = [(two, every, pl.ds(128, 128)) for two in pairs]
+
+    def b_cols(s):
+        return pl.ds(128, 384) if s < Q_FROM else pl.ds(256, 256)
+
+    bz = recv_slots(18)
+    pz, qz = [recv_slots(18) for _ in range(2)], [recv_slots(18) for _ in range(2)]
+    p0 = recv_slots(4)
+    w_own = pltpu.make_async_copy(w_ref, wbuf.at[0, x], load_sem.at[4])
+    left, right, far = (x + 3) % NX, (x + 1) % NX, (x + 2) % NX
+    rows1, rows2 = pl.ds(0, 32), pl.ds(32, 32)
+
+    def w_begin():
+        for d in (2, 1, 3):
+            copy(w_ref.at[:, pl.ds(0, 128)], wbuf.at[0, x, :, pl.ds(0, 128)], p0 + d, at_x(d))
+        copy(w_ref.at[:, b_cols(1)], wbuf.at[15, x, :, b_cols(1)], bz + 1, at_z(1))
+        copy(w_ref.at[:, b_cols(1)], wbuf.at[1, x, :, b_cols(1)], bz + 9 + 1, at_z(NZ - 1))
+        w_own.start()
+
+    def z_send(s, region, slots, to_right, to_left):
+        if to_right:
+            copy(wbuf.at[((17 - s) % NZ,) + region], wbuf.at[(16 - s,) + region], slots + s, at_z(1))
+        if to_left:
+            copy(wbuf.at[(s - 1,) + region], wbuf.at[(s,) + region], slots + 9 + s, at_z(NZ - 1))
+
+    def p_start():
+        for d in (1, 3, 2):
+            arrived(wbuf.at[0, (x + NX - d) % NX, every, pl.ds(0, 128)], p0 + d)
+        for k in (0, 1):
+            z_send(1, P_[k], pz[k], True, True)
+
+    def p_step(s):
+        for k in (0, 1):
+            a_step(s, P_[k], pz[k])
+
+    def q_start():
+        for k in (0, 1):
+            z_send(Q_FROM, Q_[k], qz[k], True, True)
+
+    def q_step(s):
+        for k in (0, 1):
+            a_step(s, Q_[k], qz[k])
+
+    def a_step(s, region, slots):
+        arrived(wbuf.at[(16 - s,) + region], slots + s)
+        if s < 8:
+            z_send(s + 1, region, slots, True, False)
+            arrived(wbuf.at[(s,) + region], slots + 9 + s)
+            z_send(s + 1, region, slots, False, s < 7)
+
+    def b_step(s):
+        if s < 8:
+            arrived(wbuf.at[16 - s, x, :, b_cols(s)], bz + s)
+            z_send(s + 1, (x, every, b_cols(s + 1)), bz, s < 7, False)
+        arrived(wbuf.at[s, x, :, b_cols(s)], bz + 9 + s)
+        z_send(s + 1, (x, every, b_cols(s + 1)), bz, False, s < 8)
+
+    slots_x = {}
+
+    def b_spans(batch):
+        lo, hi = batch[0], batch[-1]
+        n = hi - lo + 1
+        if lo == 0 or lo == 8:
+            return [(pl.ds(lo, 1), batch)]
+        return [(pl.ds(16 - hi, n), batch), (pl.ds(lo, n), batch)]
+
+    def x_send(batch):
+        cols = b_cols(batch[0])
+        for k, (o, _) in enumerate(b_spans(batch)):
+            base = slots_x[batch, k] = recv_slots(4)
+            blk = wbuf.at[o, x, :, cols]
+            copy(blk, blk, base + 0, at_x(1))
+            copy(blk, blk, base + 1, at_x(3))
+
+    def x_pass(batch):
+        cols = b_cols(batch[0])
+        for k, (o, _) in enumerate(b_spans(batch)):
+            base = slots_x[batch, k]
+            arrived(wbuf.at[o, left, :, cols], base + 0)
+            blk = wbuf.at[o, left, rows1, cols]
+            copy(blk, blk, base + 2, at_x(1))
+            arrived(wbuf.at[o, right, :, cols], base + 1)
+            blk = wbuf.at[o, right, rows2, cols]
+            copy(blk, blk, base + 3, at_x(3))
+
+    def x_end(batch):
+        cols = b_cols(batch[0])
+        for k, (o, _) in enumerate(b_spans(batch)):
+            base = slots_x[batch, k]
+            arrived(wbuf.at[o, far, rows1, cols], base + 2)
+            arrived(wbuf.at[o, far, rows2, cols], base + 3)
 
     half = (pl.ds(0, 256), pl.ds(256, 256))
     iR, iL, iF, iS = recv_slots(2), recv_slots(2), recv_slots(2), recv_slots(8)
@@ -117,14 +203,15 @@
     def ihead(d):
         return ((y + d) % NY) * 2 + c
 
-    copy(inp_ref.at[:, half[0]], inpb.at[head, :, half[0]], iR + 0, at_y(1))
-    copy(inp_ref.at[:, half[1]], inpb.at[head, :, half[1]], iL + 1, at_y(3))
-    copy(inp_ref.at[:, half[1]], inpb.at[head, :, half[1]], iR + 1, at_y(1))
-    copy(inp_ref.at[:, half[0]], inpb.at[head, :, half[0]], iL + 0, at_y(3))
-    copy(inp_ref, inpb.at[head], iS + 0, sib)
-
-    wbuf[wrows(z, x), :] = w_ref[...]
-    inpb[head] = inp_ref[...]
+    i_own = pltpu.make_async_copy(inp_ref, inpb.at[head], load_sem.at[5])
+
+    def input_begin():
+        i_own.start()
+        copy(inp_ref.at[:, half[0]], inpb.at[head, :, half[0]], iR + 0, at_y(1))
+        copy(inp_ref.at[:, half[1]], inpb.at[head, :, half[1]], iL + 1, at_y(3))
+        copy(inp_ref.at[:, half[1]], inpb.at[head, :, half[1]], iR + 1, at_y(1))
+        copy(inp_ref.at[:, half[0]], inpb.at[head, :, half[0]], iL + 0, at_y(3))
+        copy(inp_ref, inpb.at[head], iS + 0, sib)
 
     def input_pass(part):
         left, right, far = ihead(3), ihead(1), ihead(2)
@@ -145,6 +232,8 @@
                 arrived(inpb.at[far, :, half[k]], iF + k)
                 copy(inpb.at[far, :, half[k]], inpb.at[far, :, half[k]], iS + 5 + k, sib)
         if part == 3:
+            i_own.wait()
+
             def other(d):
                 return ((y + d) % NY) * 2 + (1 - c)
             arrived(inpb.at[other(0)], iS + 0)
@@ -154,72 +243,6 @@
             arrived(inpb.at[other(1), :, half[0]], iS + 4)
             for k in (0, 1):
                 arrived(inpb.at[other(2), :, half[k]], iS + 5 + k)
-
-    def w_start():
-        for d in (1, 2, 3):
-            arrived(wbuf.at[wrows(z, (x + NX - d) % NX), :], w0 + d)
-        copy(wbuf.at[wgroup(z), colsA], wbuf.at[wgroup(z), colsA], aR + 1, at_z(1))
-        copy(wbuf.at[wgroup(z), colsA], wbuf.at[wgroup(z), colsA], aL + 1, at_z(NZ - 1))
-
-    xslots = {}
-
-    def w_across(key, zz):
-        base = recv_slots(4)
-        xslots[key] = base
-        blk = wbuf.at[wrows(zz, x), colsB]
-        copy(blk, blk, base + 0, at_x(1))
-        copy(blk, blk, base + 1, at_x(3))
-
-    def w_across2(key, zz):
-        base = xslots[key]
-        left, right = (x + 3) % NX, (x + 1) % NX
-        arrived(wbuf.at[wrows(zz, left), colsB], base + 0)
-        blk = wbuf.at[wrows(zz, left), colsB1]
-        copy(blk, blk, base + 2, at_x(1))
-        arrived(wbuf.at[wrows(zz, right), colsB], base + 1)
-        blk = wbuf.at[wrows(zz, right), colsB2]
-        copy(blk, blk, base + 3, at_x(3))
-
-    def w_step(s):
-        zr_, zl_ = (z + NZ - s) % NZ, (z + s) % NZ
-        if s <= 8:
-            blk = wbuf.at[wgroup(zr_), colsA]
-            arrived(blk, aR + s)
-            if s < 8:
-                copy(blk, blk, aR + s + 1, at_z(1))
-        if s <= 7:
-            blk = wbuf.at[wgroup(zl_), colsA]
-            arrived(blk, aL + s)
-            if s < 7:
-                copy(blk, blk, aL + s + 1, at_z(NZ - 1))
-        if s <= 7:
-            blk = wbuf.at[wrows(zr_, x), colsB]
-            arrived(blk, bR + s)
-            if s < 7:
-                copy(blk, blk, bR + s + 1, at_z(1))
-            w_across(("R", s), zr_)
-        if s <= 8:
-            blk = wbuf.at[wrows(zl_, x), colsB]
-            arrived(blk, bL + s)
-            if s < 8:
-                copy(blk, blk, bL + s + 1, at_z(NZ - 1))
-            w_across(("L", s), zl_)
-        if s >= 2:
-            w_late(s - 1)
-
-    def w_late(s):
-        if s <= 7:
-            w_across2(("R", s), (z + NZ - s) % NZ)
-        if s <= 8:
-            w_across2(("L", s), (z + s) % NZ)
-
-    def w_end():
-        w_late(8)
-        far = (x + 2) % NX
-        for (side, s), base in xslots.items():
-            zz = (z + NZ - s) % NZ if side == "R" else (z + s) % NZ
-            arrived(wbuf.at[wrows(zz, far), colsB1], base + 2)
-            arrived(wbuf.at[wrows(zz, far), colsB2], base + 3)
 
     lane = iota((SPAN, 128), 1)
     low = lane < 64
@@ -281,7 +304,7 @@
 
     def scan_z_send(which):
         base = recv_slots(16)
-        for d in range(1, NZ):
+        for d in FAR_FIRST:
             to = (z + d) % NZ
             copy(tz.at[which, to], zr.at[which, z], base + d, at_z(d))
         zr[which, z] = tz[which, z]
@@ -293,7 +316,7 @@
 
     def scan_z_back(which):
         base = recv_slots(16)
-        for d in range(1, NZ):
+        for d in FAR_FIRST:
             to = (z + d) % NZ
             copy(zo.at[which, to], zp.at[which, z], base + d, at_z(d))
         zp[which, z] = zo[which, z]
@@ -332,7 +355,7 @@
             arrived(ax_ref.at[(x + NX - d) % NX], marks["ax"] + d)
         base = recv_slots(16)
         adev[4] = ax_ref[0] * ax_ref[1] * ax_ref[2] * ax_ref[3]
-        for d in range(1, NZ):
+        for d in FAR_FIRST:
             copy(adev.at[4], az_ref.at[z], base + d, at_z(d))
         az_ref[z] = adev[4]
         marks["az"] = base
@@ -419,14 +442,17 @@
         rows = pl.ds(sp * SPAN, SPAN)
         gx[rows, :] = (gxf[rows, :] + te_ref[rows, :] * mm(b_ref[rows, :], qs[sp])).astype(BF)
 
-    def project():
-        xacc[...] = jnp.zeros_like(xacc)
-
-        def one(j, carry):
-            xacc[...] += mm(inpb[j], wbuf[pl.ds(pl.multiple_of(j * 512, 512), 512), :])
+    def project(first_o, count):
+        def one(k, carry):
+            o = (first_o + k) % NZ
+            zz = (z + o) % NZ
+            cols = pl.ds(pl.multiple_of((zz % 2) * 256, 256), 256)
+            xacc[...] += mm(inpb[zz // 2, :, cols], wbuf[o].reshape(256, 512))
             return carry
 
-        lax.fori_loop(0, 8, one, 0)
+        lax.fori_loop(0, count, one, 0)
+
+    def own_states():
         xb = xacc[...].astype(BF)
         x_ref[...] = xb
         ex_ref[...] = (te_ref[...] * xb.astype(F32)).astype(BF)
@@ -438,13 +464,14 @@
 
     rS = recv_slots(4)
 
-    def wblock(j):
-        return wbuf[pl.ds(pl.multiple_of(j * 512, 512), 512), :]
+    def part_of(j, k):
+        return mm_nt(gx[...], wbuf[(2 * j + k + NZ - z) % NZ].reshape(256, 512))
 
     def rs_sib():
         for d in (2, 1, 3, 0):
             j = ((y + d) % NY) * 2 + (1 - c)
-            pbuf[j] = mm_nt(gx[...], wblock(j)).astype(BF)
+            for k in (0, 1):
+                pbuf[j, :, half[k]] = part_of(j, k).astype(BF)
             copy(pbuf.at[j], sibr.at[(y + d) % NY], rS + d, sib)
 
     rF, rN = recv_slots(2), recv_slots(4)
@@ -452,9 +479,9 @@
     def rs_own(d):
         yy = (y + d) % NY
         j = yy * 2 + c
-        own = mm_nt(gx[...], wblock(j))
         arrived(sibr.at[yy], rS + d)
-        pbuf[j] = (own + sibr[yy].astype(F32)).astype(BF)
+        for k in (0, 1):
+            pbuf[j, :, half[k]] = (part_of(j, k) + sibr[yy, :, half[k]].astype(F32)).astype(BF)
         if d == 2:
             copy(pbuf.at[j, :, half[1]], yfar.at[:, half[1]], rF + 1, at_y(1))
             copy(pbuf.at[j, :, half[0]], yfar.at[:, half[0]], rF + 0, at_y(3))
@@ -560,64 +587,128 @@
             arrived(pfull.at[which, mine((head + 8 - d) % 8), :], base + d)
         out[...] = pfull[which].astype(F32)
 
+    stores = []
+
+    def put(src, dst):
+        d = pltpu.make_async_copy(src, dst, load_sem.at[6 + len(stores)])
+        d.start()
+        stores.append(d)
+
+    w_begin()
+    input_begin()
+    for d in loads:
+        d.wait()
+    w_own.wait()
+    x_send((0,))
     first(0)
+    p_start()
+    b_step(1)
     first(1)
     ret_x()
     bscan(0)
-    w_start()
+    b_step(2)
+    x_send((1, 2))
+    xacc[...] = jnp.zeros_like(xacc)
+    p_step(1)
+    unit1(0, 0)
+    b_step(3)
+    x_send((3,))
+    x_pass((0,))
+    p_step(2)
+    unit1(0, 1)
+    b_step(4)
+    x_pass((1, 2))
+    x_end((0,))
     ret_z()
     bscan(1)
-    for s in range(1, 9):
-        unit1((s - 1) // 4, (s - 1) % 4)
-        w_step(s)
-        if s == 1:
-            bscan(2)
-        if s == 2:
-            bscan(3)
-            input_pass(0)
-        if s == 3:
-            bscan(4)
-            input_pass(1)
-        if s == 5:
-            input_pass(2)
+    input_pass(0)
+    x_pass((3,))
+    p_step(3)
+    unit1(0, 2)
+    b_step(5)
+    x_send((4, 5))
+    x_end((1, 2))
+    x_end((3,))
+    q_start()
+    p_step(4)
+    unit1(0, 3)
+    b_step(6)
+    x_send((6,))
+    x_pass((4, 5))
+    q_step(4)
+    bscan(2)
+    input_pass(1)
+    p_step(5)
+    unit1(1, 0)
+    b_step(7)
+    x_send((7,))
+    x_pass((6,))
+    q_step(5)
+    p_step(6)
+    unit1(1, 1)
+    b_step(8)
+    x_send((8,))
+    x_end((4, 5))
+    x_pass((7,))
+    q_step(6)
+    bscan(3)
+    input_pass(2)
+    p_step(7)
+    unit1(1, 2)
+    x_end((6,))
+    x_pass((8,))
+    q_step(7)
+    unit1(1, 3)
     input_pass(3)
+    project(NZ - 6, 13)
+    p_step(8)
+    x_end((7,))
+    x_end((8,))
+    q_step(8)
+    project(7, 3)
+    bscan(4)
     finish_gx(0)
     finish_gx(1)
-    w_end()
-    project()
+    own_states()
     fscan(0)
     rs_sib()
+    rs_own(2)
     fscan(1)
-    rs_own(2)
-    fscan(2)
     rs_own(1)
     rs_own(3)
     rs_own(0)
-    fscan(3)
     unit2(0)
+    fscan(2)
+    unit2(1)
     rs_pass()
-    unit2(1)
     grad_b_part(0)
     grad_b_part(1)
     pb = ps_send(0)
+    fscan(3)
+    pb = ps_sum(0, pb)
     fscan(4)
     grad_c_part(0)
     grad_c_part(1)
     pc = ps_send(1)
-    pb = ps_sum(0, pb)
     decay_part(0)
     pc = ps_sum(1, pc)
     decay_part(1)
+    put(gld_ref, gld_hbm)
     ps_end(0, pb, gb_ref)
+    put(gb_ref, gb_hbm)
+    rs_end()
+    put(gi_ref, gi_hbm)
     ps_end(1, pc, gc_ref)
-    rs_end()
+    put(gc_ref, gc_hbm)
+    for d in stores:
+        d.wait()
     for d in sent:
         d.wait_send()
     assert counts["s"] <= N_SEND and counts["r"] <= N_RECV, counts
 
 
 def local(inputs, w_in, b_rows, c_rows, log_decay, skip_gain, grad_out):
-    vmem = pl.BlockSpec(memory_space=pltpu.VMEM)
+    hbm = pl.BlockSpec(memory_space=pl.ANY)
     V = pltpu.VMEM
     return pl.pallas_call(
         kernel,
@@ -627,10 +718,18 @@
             jax.ShapeDtypeStruct((T, 128), F32),
             jax.ShapeDtypeStruct((8, T), F32),
         ),
-        in_specs=[vmem] * 5 + [pl.BlockSpec(memory_space=pltpu.SMEM), vmem],
-        out_specs=(vmem,) * 4,
+        in_specs=[hbm] * 5 + [pl.BlockSpec(memory_space=pltpu.SMEM), hbm],
+        out_specs=(hbm,) * 4,
         scratch_shapes=[
-            V((4096, 512), BF),
+            V((T, 128), BF),
+            V((T, 128), BF),
+            V((8, T), F32),
+            V((T, 512), BF),
+            V((T, 512), BF),
+            V((T, 128), F32),
+            V((T, 128), F32),
+            V((8, T), F32),
+            V((NZ, NX, 64, 512), BF),
             V((8, T, 512), BF),
             V((8, T, 512), BF),
             V((4, T, 512), BF),
@@ -672,9 +771,10 @@
             V((2, T, 128), BF),
             pltpu.SemaphoreType.DMA((N_SEND,)),
             pltpu.SemaphoreType.DMA((N_RECV,)),
+            pltpu.SemaphoreType.DMA((10,)),
         ],
         compiler_params=pltpu.CompilerParams(
-            collective_id=0, has_side_effects=True, vmem_limit_bytes=52 * 1024 * 1024
+            collective_id=0, has_side_effects=True, vmem_limit_bytes=60 * 1024 * 1024
         ),
         cost_estimate=pl.CostEstimate(flops=8 * 10**9, bytes_accessed=4 * 10**6, transcendentals=2 * 10**6),
     )(inputs, w_in, b_rows, c_rows, log_decay, skip_gain, grad_out)

time: 127 us -> 110 us (0.87)
  Pallas kernels: 118 us -> 105 us
  local copies, waits for them, and re-layouts: 7.86 us -> 4.28 us
    pallas_call x1, Pallas kernels: 118 us -> 105 us  [local(): pl.pallas_call(kernel, out_shape=(jax.ShapeDtypeStruct((T, 512), BF), jax...]
    unnamed x16 -> x10, local copies, waits for them, and re-layouts: 7.86 us -> 4.28 us
where the time goes in v2:
time: 110 us
  Pallas kernels  105 us (95%)
  local copies, waits for them, and re-layouts  4.28 us (4%)
    pallas_call x1, Pallas kernels, local(): pl.pallas_call(kernel, out_shape=(jax.ShapeDtypeStruct((T, 512), BF), jax...  105 us
    unnamed x10, local copies, waits for them, and re-layouts  4.28 us

profile of v2, /device:TPU:1, one launch (start us, length us, event | category | flops | bytes accessed | tf_op | source)
XLA Modules:
  0.0 109.8 jit_solution(18024357497804362921)
XLA Ops:
  0.6 104.9 %shard_map.102 = (bf16[512,512]{1,0:T(8,128)(2,1)}, f32[512,128]{1,0:T(8,128)}, f32[512,128]{1,0:T(8,128)}, f32[8,512]{1,0:T(8,128)}) custom-call(bf16[512,512]{1,0:T(8,128)(2,1)} %inp_ref.1, bf16[64,512]{1,0:T(8,128)(2,1)} %w_ref.1, bf16[512,128]{1,0:T(8,128)(2,1)} %b_hbm.1, bf16[512,128]{1,0:T(8,128)(2,1)} %c_hbm.1, f32[8,512]{1,0:T(8,128)} %ld_hbm.1, ...), custom_call_target="tpu_custom_call" | custom-call | flops 8000000000 | bytes 4000000 | tf_op jit(solution)/shard_map/pallas_call | solution.py:713
  105.5 0.0 copy-start.1
  105.5 1.9 %copy.15 = bf16[512,512]{1,0:T(8,128)(2,1)} copy(bf16[512,512]{1,0:T(8,128)(2,1)} %get-tuple-element.8) | data formatting | bytes 1048576
  107.5 0.0 copy-done.1
  107.5 0.0 copy-start
  107.5 0.7 copy.16
  108.2 0.3 copy-done
  108.5 0.0 copy-start.2
  108.5 0.7 copy.17
  109.2 0.0 copy-done.2
  109.2 0.6 copy.18
Async XLA Ops:
  105.5 1.9 %copy-start.1 = (f32[512,128]{1,0:T(8,128)S(1)}, f32[512,128]{1,0:T(8,128)}, u32[]{:S(2)}) copy-start(f32[512,128]{1,0:T(8,128)} %get-tuple-element.9) | copy-start | bytes 786436
  107.5 1.0 copy-start
  108.5 0.7 copy-start.2

commit v3 on v2

--- a/solution.py
+++ b/solution.py
@@ -467,12 +467,11 @@
     def part_of(j, k):
         return mm_nt(gx[...], wbuf[(2 * j + k + NZ - z) % NZ].reshape(256, 512))
 
-    def rs_sib():
-        for d in (2, 1, 3, 0):
-            j = ((y + d) % NY) * 2 + (1 - c)
-            for k in (0, 1):
-                pbuf[j, :, half[k]] = part_of(j, k).astype(BF)
-            copy(pbuf.at[j], sibr.at[(y + d) % NY], rS + d, sib)
+    def rs_sib(d):
+        j = ((y + d) % NY) * 2 + (1 - c)
+        for k in (0, 1):
+            pbuf[j, :, half[k]] = part_of(j, k).astype(BF)
+        copy(pbuf.at[j], sibr.at[(y + d) % NY], rS + d, sib)
 
     rF, rN = recv_slots(2), recv_slots(4)
 
@@ -541,11 +540,13 @@
         rows = pl.ds(sp * SPAN, SPAN)
         pr[0, rows, :] = (mm(dmt[sp].astype(BF), c_ref[rows, :]) + mm_nt(ex_ref[rows, :], qs[sp])).astype(BF)
 
+    def grad_c_inner(sp):
+        rows = pl.ds(sp * SPAN, SPAN)
+        gc_ref[rows, :] = mm_tn(dmt[sp].astype(BF), b_ref[rows, :])
+
     def grad_c_part(sp):
         rows = pl.ds(sp * SPAN, SPAN)
-        pr[1, rows, :] = (
-            mm_tn(dmt[sp].astype(BF), b_ref[rows, :]) + mm_nt(v_ref[rows, :], ss[sp])
-        ).astype(BF)
+        pr[1, rows, :] = (gc_ref[rows, :] + mm_nt(v_ref[rows, :], ss[sp])).astype(BF)
 
     def decay_part(sp):
         rows = pl.ds(sp * SPAN, SPAN)
@@ -666,24 +667,29 @@
     x_end((8,))
     q_step(8)
     project(7, 3)
+    own_states()
+    fscan(0)
     bscan(4)
     finish_gx(0)
     finish_gx(1)
-    own_states()
-    fscan(0)
-    rs_sib()
+    rs_sib(2)
+    rs_sib(1)
     rs_own(2)
     fscan(1)
+    rs_sib(3)
     rs_own(1)
+    rs_sib(0)
     rs_own(3)
     rs_own(0)
     unit2(0)
     fscan(2)
     unit2(1)
-    rs_pass()
     grad_b_part(0)
     grad_b_part(1)
     pb = ps_send(0)
+    grad_c_inner(0)
+    grad_c_inner(1)
+    rs_pass()
     fscan(3)
     pb = ps_sum(0, pb)
     fscan(4)

time: 110 us -> 107 us (0.973)
  Pallas kernels: 105 us -> 102 us
    pallas_call x1, Pallas kernels: 105 us -> 102 us  [local(): pl.pallas_call(kernel, out_shape=(jax.ShapeDtypeStruct((T, 512), BF), jax...]
where the time goes in v3:
time: 107 us
  Pallas kernels  102 us (95%)
  local copies, waits for them, and re-layouts  4.28 us (4%)
    pallas_call x1, Pallas kernels, local(): pl.pallas_call(kernel, out_shape=(jax.ShapeDtypeStruct((T, 512), BF), jax...  102 us
    unnamed x10, local copies, waits for them, and re-layouts  4.28 us

profile of v3, /device:TPU:1, one launch (start us, length us, event | category | flops | bytes accessed | tf_op | source)
XLA Modules:
  0.0 106.5 jit_solution(7071176802416242519)
XLA Ops:
  0.6 101.6 %shard_map.102 = (bf16[512,512]{1,0:T(8,128)(2,1)}, f32[512,128]{1,0:T(8,128)}, f32[512,128]{1,0:T(8,128)}, f32[8,512]{1,0:T(8,128)}) custom-call(bf16[512,512]{1,0:T(8,128)(2,1)} %inp_ref.1, bf16[64,512]{1,0:T(8,128)(2,1)} %w_ref.1, bf16[512,128]{1,0:T(8,128)(2,1)} %b_hbm.1, bf16[512,128]{1,0:T(8,128)(2,1)} %c_hbm.1, f32[8,512]{1,0:T(8,128)} %ld_hbm.1, ...), custom_call_target="tpu_custom_call" | custom-call | flops 8000000000 | bytes 4000000 | tf_op jit(solution)/shard_map/pallas_call | solution.py:719
  102.2 0.0 copy-start.1
  102.2 1.9 %copy.15 = bf16[512,512]{1,0:T(8,128)(2,1)} copy(bf16[512,512]{1,0:T(8,128)(2,1)} %get-tuple-element.8) | data formatting | bytes 1048576
  104.2 0.0 copy-done.1
  104.2 0.0 copy-start
  104.2 0.7 copy.16
  104.9 0.3 copy-done
  105.2 0.0 copy-start.2
  105.2 0.7 copy.17
  105.9 0.0 copy-done.2
  105.9 0.6 copy.18
Async XLA Ops:
  102.2 1.9 %copy-start.1 = (f32[512,128]{1,0:T(8,128)S(1)}, f32[512,128]{1,0:T(8,128)}, u32[]{:S(2)}) copy-start(f32[512,128]{1,0:T(8,128)} %get-tuple-element.9) | copy-start | bytes 786436
  104.2 1.0 copy-start
  105.2 0.7 copy-start.2

commit v4 on v3

--- a/solution.py
+++ b/solution.py
@@ -33,8 +33,8 @@
     return lax.broadcasted_iota(jnp.int32, shape, dim)
 
 
-N_SEND = 300
-N_RECV = 340
+N_SEND = 48
+N_RECV = 137
 
 
 def kernel(
@@ -77,8 +77,10 @@
     def copy(src, dst, slot, device):
         k = counts["s"]
         counts["s"] += 1
+        if k >= N_SEND:
+            sent[k - N_SEND].wait_send()
         d = pltpu.make_async_remote_copy(
-            src_ref=src, dst_ref=dst, send_sem=send_sem.at[k], recv_sem=recv_sem.at[slot],
+            src_ref=src, dst_ref=dst, send_sem=send_sem.at[k % N_SEND], recv_sem=recv_sem.at[slot],
             device_id=device, device_id_type=MESH,
         )
         d.start()
@@ -110,29 +112,29 @@
     def b_cols(s):
         return pl.ds(128, 384) if s < Q_FROM else pl.ds(256, 256)
 
-    bz = recv_slots(18)
-    pz, qz = [recv_slots(18) for _ in range(2)], [recv_slots(18) for _ in range(2)]
-    p0 = recv_slots(4)
+    bz = (recv_slots(7) - 1, recv_slots(8) - 1)
+    pz = [(recv_slots(8) - 1, recv_slots(7) - 1) for _ in range(2)]
+    qz = [(recv_slots(9 - Q_FROM) - Q_FROM, recv_slots(8 - Q_FROM) - Q_FROM) for _ in range(2)]
+    p0 = recv_slots(1)
     w_own = pltpu.make_async_copy(w_ref, wbuf.at[0, x], load_sem.at[4])
     left, right, far = (x + 3) % NX, (x + 1) % NX, (x + 2) % NX
     rows1, rows2 = pl.ds(0, 32), pl.ds(32, 32)
 
     def w_begin():
         for d in (2, 1, 3):
-            copy(w_ref.at[:, pl.ds(0, 128)], wbuf.at[0, x, :, pl.ds(0, 128)], p0 + d, at_x(d))
-        copy(w_ref.at[:, b_cols(1)], wbuf.at[15, x, :, b_cols(1)], bz + 1, at_z(1))
-        copy(w_ref.at[:, b_cols(1)], wbuf.at[1, x, :, b_cols(1)], bz + 9 + 1, at_z(NZ - 1))
+            copy(w_ref.at[:, pl.ds(0, 128)], wbuf.at[0, x, :, pl.ds(0, 128)], p0, at_x(d))
+        copy(w_ref.at[:, b_cols(1)], wbuf.at[15, x, :, b_cols(1)], bz[0] + 1, at_z(1))
+        copy(w_ref.at[:, b_cols(1)], wbuf.at[1, x, :, b_cols(1)], bz[1] + 1, at_z(NZ - 1))
         w_own.start()
 
     def z_send(s, region, slots, to_right, to_left):
         if to_right:
-            copy(wbuf.at[((17 - s) % NZ,) + region], wbuf.at[(16 - s,) + region], slots + s, at_z(1))
+            copy(wbuf.at[((17 - s) % NZ,) + region], wbuf.at[(16 - s,) + region], slots[0] + s, at_z(1))
         if to_left:
-            copy(wbuf.at[(s - 1,) + region], wbuf.at[(s,) + region], slots + 9 + s, at_z(NZ - 1))
+            copy(wbuf.at[(s - 1,) + region], wbuf.at[(s,) + region], slots[1] + s, at_z(NZ - 1))
 
     def p_start():
-        for d in (1, 3, 2):
-            arrived(wbuf.at[0, (x + NX - d) % NX, every, pl.ds(0, 128)], p0 + d)
+        arrived(wbuf.at[0, pl.ds(0, 3), every, pl.ds(0, 128)], p0)
         for k in (0, 1):
             z_send(1, P_[k], pz[k], True, True)
 
@@ -149,17 +151,17 @@
             a_step(s, Q_[k], qz[k])
 
     def a_step(s, region, slots):
-        arrived(wbuf.at[(16 - s,) + region], slots + s)
+        arrived(wbuf.at[(16 - s,) + region], slots[0] + s)
         if s < 8:
             z_send(s + 1, region, slots, True, False)
-            arrived(wbuf.at[(s,) + region], slots + 9 + s)
+            arrived(wbuf.at[(s,) + region], slots[1] + s)
             z_send(s + 1, region, slots, False, s < 7)
 
     def b_step(s):
         if s < 8:
-            arrived(wbuf.at[16 - s, x, :, b_cols(s)], bz + s)
+            arrived(wbuf.at[16 - s, x, :, b_cols(s)], bz[0] + s)
             z_send(s + 1, (x, every, b_cols(s + 1)), bz, s < 7, False)
-        arrived(wbuf.at[s, x, :, b_cols(s)], bz + 9 + s)
+        arrived(wbuf.at[s, x, :, b_cols(s)], bz[1] + s)
         z_send(s + 1, (x, every, b_cols(s + 1)), bz, False, s < 8)
 
     slots_x = {}
@@ -174,7 +176,7 @@
     def x_send(batch):
         cols = b_cols(batch[0])
         for k, (o, _) in enumerate(b_spans(batch)):
-            base = slots_x[batch, k] = recv_slots(4)
+            base = slots_x[batch, k] = recv_slots(3)
             blk = wbuf.at[o, x, :, cols]
             copy(blk, blk, base + 0, at_x(1))
             copy(blk, blk, base + 1, at_x(3))
@@ -188,17 +190,16 @@
             copy(blk, blk, base + 2, at_x(1))
             arrived(wbuf.at[o, right, :, cols], base + 1)
             blk = wbuf.at[o, right, rows2, cols]
-            copy(blk, blk, base + 3, at_x(3))
+            copy(blk, blk, base + 2, at_x(3))
 
     def x_end(batch):
         cols = b_cols(batch[0])
         for k, (o, _) in enumerate(b_spans(batch)):
             base = slots_x[batch, k]
-            arrived(wbuf.at[o, far, rows1, cols], base + 2)
-            arrived(wbuf.at[o, far, rows2, cols], base + 3)
+            arrived(wbuf.at[o, far, :, cols], base + 2)
 
     half = (pl.ds(0, 256), pl.ds(256, 256))
-    iR, iL, iF, iS = recv_slots(2), recv_slots(2), recv_slots(2), recv_slots(8)
+    iR, iL, iF, iS = recv_slots(2), recv_slots(2), recv_slots(2), recv_slots(7)
 
     def ihead(d):
         return ((y + d) % NY) * 2 + c
@@ -289,80 +290,74 @@
         gxf[rows, cols] = jnp.where(low, parts[0], parts[1]) + skip * g2.astype(F32)
 
     def scan_x_send(which, state):
-        base = recv_slots(4)
+        base = recv_slots(1)
         for i in range(4):
             sx_ref[which, i] = state(i).astype(BF)
         for d in (1, 3, 2):
             to = (x + d) % NX
-            copy(sx_ref.at[which, to], xr.at[which, x], base + d, at_x(d))
+            copy(sx_ref.at[which, to], xr.at[which, x], base, at_x(d))
         xr[which, x] = sx_ref[which, x]
         return base
 
     def scan_x_wait(which, base):
-        for d in (1, 2, 3):
-            arrived(xr.at[which, (x + NX - d) % NX], base + d)
+        arrived(xr.at[which, pl.ds(0, NX - 1)], base)
 
     def scan_z_send(which):
-        base = recv_slots(16)
+        base = recv_slots(1)
         for d in FAR_FIRST:
             to = (z + d) % NZ
-            copy(tz.at[which, to], zr.at[which, z], base + d, at_z(d))
+            copy(tz.at[which, to], zr.at[which, z], base, at_z(d))
         zr[which, z] = tz[which, z]
         return base
 
     def scan_z_wait(which, base):
-        for d in range(1, NZ):
-            arrived(zr.at[which, (z + NZ - d) % NZ], base + d)
+        arrived(zr.at[which, pl.ds(0, NZ - 1)], base)
 
     def scan_z_back(which):
-        base = recv_slots(16)
+        base = recv_slots(1)
         for d in FAR_FIRST:
             to = (z + d) % NZ
-            copy(zo.at[which, to], zp.at[which, z], base + d, at_z(d))
+            copy(zo.at[which, to], zp.at[which, z], base, at_z(d))
         zp[which, z] = zo[which, z]
         return base
 
     def scan_z_back_wait(which, base):
-        for d in range(1, NZ):
-            arrived(zp.at[which, (z + NZ - d) % NZ], base + d)
+        arrived(zp.at[which, pl.ds(0, NZ - 1)], base)
 
     def scan_x_back(which):
-        base = recv_slots(4)
+        base = recv_slots(1)
         for d in (1, 3, 2):
             to = (x + d) % NX
-            copy(bo_ref.at[which, to], br_ref.at[which, x], base + d, at_x(d))
+            copy(bo_ref.at[which, to], br_ref.at[which, x], base, at_x(d))
         br_ref[which, x] = bo_ref[which, x]
         return base
 
     def scan_x_back_wait(which, base):
-        for d in (1, 2, 3):
-            arrived(br_ref.at[which, (x + NX - d) % NX], base + d)
+        arrived(br_ref.at[which, pl.ds(0, NX - 1)], base)
 
     marks = {}
 
     def ret_x():
-        base = recv_slots(4)
+        base = recv_slots(1)
         for i in range(4):
             adev[i] = a_ref[0, i] * a_ref[1, i]
         for d in (1, 3, 2):
             to = (x + d) % NX
-            copy(adev.at[to], ax_ref.at[x], base + d, at_x(d))
+            copy(adev.at[to], ax_ref.at[x], base, at_x(d))
         ax_ref[x] = adev[x]
         marks["ax"] = base
 
     def ret_z():
-        for d in (1, 2, 3):
-            arrived(ax_ref.at[(x + NX - d) % NX], marks["ax"] + d)
-        base = recv_slots(16)
+        arrived(ax_ref.at[pl.ds(0, NX - 1)], marks["ax"])
+        base = recv_slots(1)
         adev[4] = ax_ref[0] * ax_ref[1] * ax_ref[2] * ax_ref[3]
         for d in FAR_FIRST:
-            copy(adev.at[4], az_ref.at[z], base + d, at_z(d))
+            copy(adev.at[4], az_ref.at[z], base, at_z(d))
         az_ref[z] = adev[4]
         marks["az"] = base
 
     def ret_wait():
-        for d in range(1, NZ):
-            arrived(az_ref.at[(z + NZ - d) % NZ], marks["az"] + d)
+        arrived(az_ref.at[pl.ds(0, NZ - 1)], marks["az"])
 
     def ret(k):
         return ax_ref[k][0:1, :]
@@ -563,29 +558,27 @@
         return pl.ds(pl.multiple_of(k * 64, 64), 64)
 
     def ps_send(which):
-        base = recv_slots(8)
-        for d in range(1, 8):
+        base = recv_slots(1)
+        for d in (4, 3, 5, 2, 6, 1, 7):
             to = (head + d) % 8
-            copy(pr.at[which, mine(to), :], prr.at[which, head], base + d, at_head(d))
+            copy(pr.at[which, mine(to), :], prr.at[which, head], base, at_head(d))
         prr[which, head] = pr[which, mine(head), :]
         return base
 
     def ps_sum(which, base):
-        for d in range(1, 8):
-            arrived(prr.at[which, (head + 8 - d) % 8], base + d)
+        arrived(prr.at[which, pl.ds(0, 7)], base)
         total = prr[which, 0].astype(F32)
         for k in range(1, 8):
             total = total + prr[which, k].astype(F32)
         pfin[which] = total.astype(BF)
-        base = recv_slots(8)
-        for d in range(1, 8):
-            copy(pfin.at[which], pfull.at[which, mine(head), :], base + d, at_head(d))
+        base = recv_slots(1)
+        for d in (4, 3, 5, 2, 6, 1, 7):
+            copy(pfin.at[which], pfull.at[which, mine(head), :], base, at_head(d))
         pfull[which, mine(head), :] = pfin[which]
         return base
 
     def ps_end(which, base, out):
-        for d in range(1, 8):
-            arrived(pfull.at[which, mine((head + 8 - d) % 8), :], base + d)
+        arrived(pfull.at[which, pl.ds(0, 448), :], base)
         out[...] = pfull[which].astype(F32)
 
     stores = []
@@ -708,9 +701,9 @@
     put(gc_ref, gc_hbm)
     for d in stores:
         d.wait()
-    for d in sent:
+    for d in sent[-N_SEND:]:
         d.wait_send()
-    assert counts["s"] <= N_SEND and counts["r"] <= N_RECV, counts
+    assert counts["r"] == N_RECV, counts
 
 
 def local(inputs, w_in, b_rows, c_rows, log_decay, skip_gain, grad_out):

time: 107 us -> 102 us (0.953)
  Pallas kernels: 102 us -> 96.9 us
    pallas_call x1, Pallas kernels: 102 us -> 96.9 us  [local(): pl.pallas_call(kernel, out_shape=(jax.ShapeDtypeStruct((T, 512), BF), jax...]
where the time goes in v4:
time: 102 us
  Pallas kernels  96.9 us (95%)
  local copies, waits for them, and re-layouts  4.28 us (4%)
    pallas_call x1, Pallas kernels, local(): pl.pallas_call(kernel, out_shape=(jax.ShapeDtypeStruct((T, 512), BF), jax...  96.9 us
    unnamed x10, local copies, waits for them, and re-layouts  4.28 us

profile of v4, /device:TPU:1, one launch (start us, length us, event | category | flops | bytes accessed | tf_op | source)
XLA Modules:
  0.0 101.8 jit_solution(8427829317668833022)
XLA Ops:
  0.6 96.9 %shard_map.102 = (bf16[512,512]{1,0:T(8,128)(2,1)}, f32[512,128]{1,0:T(8,128)}, f32[512,128]{1,0:T(8,128)}, f32[8,512]{1,0:T(8,128)}) custom-call(bf16[512,512]{1,0:T(8,128)(2,1)} %inp_ref.1, bf16[64,512]{1,0:T(8,128)(2,1)} %w_ref.1, bf16[512,128]{1,0:T(8,128)(2,1)} %b_hbm.1, bf16[512,128]{1,0:T(8,128)(2,1)} %c_hbm.1, f32[8,512]{1,0:T(8,128)} %ld_hbm.1, ...), custom_call_target="tpu_custom_call" | custom-call | flops 8000000000 | bytes 4000000 | tf_op jit(solution)/shard_map/pallas_call | solution.py:712
  97.5 0.0 copy-start.1
  97.5 1.9 %copy.15 = bf16[512,512]{1,0:T(8,128)(2,1)} copy(bf16[512,512]{1,0:T(8,128)(2,1)} %get-tuple-element.8) | data formatting | bytes 1048576
  99.4 0.0 copy-done.1
  99.4 0.0 copy-start
  99.4 0.7 copy.16
  100.1 0.3 copy-done
  100.5 0.0 copy-start.2
  100.5 0.7 copy.17
  101.2 0.0 copy-done.2
  101.2 0.6 copy.18
Async XLA Ops:
  97.5 1.9 %copy-start.1 = (f32[512,128]{1,0:T(8,128)S(1)}, f32[512,128]{1,0:T(8,128)}, u32[]{:S(2)}) copy-start(f32[512,128]{1,0:T(8,128)} %get-tuple-element.9) | copy-start | bytes 786436
  99.4 1.0 %copy-start = (f32[512,128]{1,0:T(8,128)S(1)}, f32[512,128]{1,0:T(8,128)}, u32[]{:S(2)}) copy-start(f32[512,128]{1,0:T(8,128)} %get-tuple-element.10) | copy-start | bytes 786436
  100.5 0.7 copy-start.2

commit v5 on v4

--- a/solution.py
+++ b/solution.py
@@ -33,7 +33,7 @@
     return lax.broadcasted_iota(jnp.int32, shape, dim)
 
 
-N_SEND = 48
+N_SEND = 32
 N_RECV = 137
 
 
@@ -401,8 +401,6 @@
                 qs[0, :, cols] = (gst[1, i] + a_ref[1, i][0:1, :] * q.astype(F32)).astype(BF)
 
     def fscan(part):
-        if part == 0:
-            marks["f0"] = scan_x_send(1, lambda i: a_ref[1, i][0:1, :] * est[0, i] + est[1, i])
         if part == 1:
             scan_x_wait(1, marks["f0"])
             total = xr[1, 0].astype(F32)
@@ -450,12 +448,19 @@
     def own_states():
         xb = xacc[...].astype(BF)
         x_ref[...] = xb
-        ex_ref[...] = (te_ref[...] * xb.astype(F32)).astype(BF)
-        for sp in range(2):
-            rows = pl.ds(sp * SPAN, SPAN)
-            bt = b_ref[rows, :].T
-            for i in range(4):
-                est[sp, i] = mm(bt, ex_ref[rows, pl.ds(i * 128, 128)])
+        bt = [b_ref[pl.ds(sp * SPAN, SPAN), :].T for sp in range(2)]
+        marks["f0"] = recv_slots(1)
+        for d in (2, 1, 3, 0):
+            to = (x + d) % NX
+            cols = pl.ds(pl.multiple_of(to * 128, 128), 128)
+            ex_ref[:, cols] = (te_ref[:, cols] * x_ref[:, cols].astype(F32)).astype(BF)
+            for sp in range(2):
+                est[sp, to] = mm(bt[sp], ex_ref[pl.ds(sp * SPAN, SPAN), cols])
+            sx_ref[1, to] = (a_ref[1, to][0:1, :] * est[0, to] + est[1, to]).astype(BF)
+            if d:
+                copy(sx_ref.at[1, to], xr.at[1, x], marks["f0"], at_x(d))
+            else:
+                xr[1, x] = sx_ref[1, x]
 
     rS = recv_slots(4)
 
@@ -661,7 +666,6 @@
     q_step(8)
     project(7, 3)
     own_states()
-    fscan(0)
     bscan(4)
     finish_gx(0)
     finish_gx(1)

time: 102 us -> 102 us (level)
  no operation moved by 1% of the time
where the time goes in v5:
time: 102 us
  Pallas kernels  96.7 us (95%)
  local copies, waits for them, and re-layouts  4.28 us (4%)
    pallas_call x1, Pallas kernels, local(): pl.pallas_call(kernel, out_shape=(jax.ShapeDtypeStruct((T, 512), BF), jax...  96.7 us
    unnamed x10, local copies, waits for them, and re-layouts  4.28 us

profile of v5, /device:TPU:1, one launch (start us, length us, event | category | flops | bytes accessed | tf_op | source)
XLA Modules:
  0.0 101.7 jit_solution(10620349415746084902)
XLA Ops:
  0.6 96.7 %shard_map.102 = (bf16[512,512]{1,0:T(8,128)(2,1)}, f32[512,128]{1,0:T(8,128)}, f32[512,128]{1,0:T(8,128)}, f32[8,512]{1,0:T(8,128)}) custom-call(bf16[512,512]{1,0:T(8,128)(2,1)} %inp_ref.1, bf16[64,512]{1,0:T(8,128)(2,1)} %w_ref.1, bf16[512,128]{1,0:T(8,128)(2,1)} %b_hbm.1, bf16[512,128]{1,0:T(8,128)(2,1)} %c_hbm.1, f32[8,512]{1,0:T(8,128)} %ld_hbm.1, ...), custom_call_target="tpu_custom_call" | custom-call | flops 8000000000 | bytes 4000000 | tf_op jit(solution)/shard_map/pallas_call | solution.py:716
  97.4 0.0 copy-start.1
  97.4 1.9 %copy.15 = bf16[512,512]{1,0:T(8,128)(2,1)} copy(bf16[512,512]{1,0:T(8,128)(2,1)} %get-tuple-element.8) | data formatting | bytes 1048576
  99.3 0.0 copy-done.1
  99.3 0.0 copy-start
  99.3 0.7 copy.16
  100.0 0.3 copy-done
  100.3 0.0 copy-start.2
  100.3 0.7 copy.17
  101.1 0.0 copy-done.2
  101.1 0.6 copy.18
Async XLA Ops:
  97.4 1.9 %copy-start.1 = (f32[512,128]{1,0:T(8,128)S(1)}, f32[512,128]{1,0:T(8,128)}, u32[]{:S(2)}) copy-start(f32[512,128]{1,0:T(8,128)} %get-tuple-element.9) | copy-start | bytes 786436
  99.3 1.0 %copy-start = (f32[512,128]{1,0:T(8,128)S(1)}, f32[512,128]{1,0:T(8,128)}, u32[]{:S(2)}) copy-start(f32[512,128]{1,0:T(8,128)} %get-tuple-element.10) | copy-start | bytes 786436
  100.3 0.7 copy-start.2
